TPU v7x, 32 devices: a whole 2x2x4 slice. The times are simulated.
32 devices in a mesh: dp: 8 (over z, core), tensor: 4 (over y, x).
Axes of the slice: x: 2, y: 2, z: 4, core: 2. Of those that a mesh axis runs over, the one named last changes fastest.
Arguments:
- hidden: bfloat16 [2048, 4096], P(('dp', 'tensor')), may hold values from -3.6 to 3.6
- lengths: int32 [8, 32], P('dp'), may hold values from 1 to 80, 256 in all within a row
- positives: int32 [64], replicated, may hold values from 0 to 191, as said below
- negatives: int32 [64, 7], replicated, may hold values from 1 to 190, as said below
- in_gain: float32 [4096], replicated, may hold values from 0.25 to 1.75
- wq: bfloat16 [4096, 512], P(None, 'tensor'), may hold values from -0.09375 to 0.09375
- wkv: bfloat16 [4096, 512], P(None, 'tensor'), may hold values from -0.09375 to 0.09375
- q_gain: float32 [128], replicated, may hold values from 0.25 to 1.75
- k_gain: float32 [128], replicated, may hold values from 0.25 to 1.75
- wo: bfloat16 [512, 4096], P('tensor'), may hold values from -0.25 to 0.25
- out_gain: float32 [4096], replicated, may hold values from 0.25 to 1.75
Outputs:
- d_hidden: bfloat16 [2048, 4096], P(('dp', 'tensor'))
- loss: float32 [], replicated
Inputs may be any that keep to these rules, and one draw needn't show every extreme that they name: Each group's 32 lengths sum to 256, and one of them is exactly 80. The 64 positives are distinct passages. The 7 hard negatives of a query are distinct, and none of them is any query's positive.
All inputs are finite; a program needn't handle non-finite values.
Results may differ from a plain program's by a relative error of at most 0.023.
Values may be sent and summed in bfloat16 or wider, within the bound.
A program may use at most 64 MiB of HBM per device.

v0:
```python
import math

import jax
import jax.numpy as jnp
from jax import lax
from jax.sharding import PartitionSpec as P

QDEV = 8


EPSILON = 1e-06
SOFTMAX_TEMPER = 0.05
LOSS_MULTIPLIER = 8192.0
ROPE_BASE = 1000000.0


def swapped(value, axis, apart):
    mask = 2**apart
    pairs = [(source, source ^ mask) for source in range(lax.axis_size(axis))]
    return lax.ppermute(value, axis, pairs)


def rms_scale(tensor):
    return lax.rsqrt(jnp.mean(tensor * tensor, axis=-1, keepdims=True) + EPSILON)


def rope_tables(position, head_width):
    halfway = head_width // 2
    frequency = ROPE_BASE ** (-(jnp.arange(halfway, dtype=jnp.float32) * (2.0 / head_width)))
    angles = position[:, None] * frequency[None, :]
    angles = jnp.concatenate([angles, angles], axis=-1)
    return (jnp.cos(angles), jnp.sin(angles))


def rotate(tensor, cosine, sine):
    halfway = tensor.shape[-1] // 2
    turned = jnp.concatenate([-tensor[..., halfway:], tensor[..., :halfway]], axis=-1)
    return tensor * cosine + turned * sine


def segment_layout(lengths_row, total_tokens):
    seq_ends = jnp.cumsum(lengths_row)
    starts = seq_ends - lengths_row
    token_index = jnp.arange(total_tokens, dtype=jnp.int32)
    inside = (token_index[:, None] >= starts[None, :]) & (token_index[:, None] < seq_ends[None, :])
    offset = jnp.sum(jnp.where(inside, starts[None, :], 0), axis=1)
    position = (token_index - offset).astype(jnp.float32)
    return (inside, position, seq_ends - 1)


def head_forward(raw, gain, cosine, sine):
    inverse = rms_scale(raw)
    unit_form = raw * inverse
    return (unit_form, inverse, rotate(unit_form * gain, cosine, sine))


def norm_backward(grad, unit_form, inverse, gain):
    scaled = grad * gain
    return inverse * (scaled - unit_form * jnp.mean(unit_form * scaled, axis=-1, keepdims=True))


def head_backward(grad_rot, unit_form, inverse, gain, cosine, sine):
    return norm_backward(rotate(grad_rot, cosine, -sine), unit_form, inverse, gain)


def contrast(embeds16, positives, negatives):
    groups = embeds16.shape[0]
    feature_count = embeds16.shape[2]
    query_rows = embeds16[:, :QDEV].reshape(groups * QDEV, feature_count)
    passage_rows = embeds16[:, QDEV:].reshape(-1, feature_count)
    query_total_count = query_rows.shape[0]
    passage_ids = jnp.arange(passage_rows.shape[0], dtype=jnp.int32)
    similarity_logits = (
        jnp.dot(query_rows, passage_rows.T, preferred_element_type=jnp.float32) / SOFTMAX_TEMPER
    )
    positive_hot = positives[:, None] == passage_ids[None, :]
    hard_hot = jnp.any(negatives[:, :, None] == passage_ids[None, None, :], axis=1)
    permitted_mask = jnp.any(positive_hot, axis=0)[None, :] | hard_hot
    weight_params = jnp.where(
        permitted_mask, jnp.exp(similarity_logits - 1.0 / SOFTMAX_TEMPER), 0.0
    )
    running_totals = jnp.sum(weight_params, axis=1, keepdims=True)
    target_labels = jnp.sum(jnp.where(positive_hot, similarity_logits, 0.0), axis=1)
    loss = jnp.mean(jnp.log(running_totals[:, 0]) + 1.0 / SOFTMAX_TEMPER - target_labels)
    scaling_factor = LOSS_MULTIPLIER / (query_total_count * SOFTMAX_TEMPER)
    coef16 = (
        scaling_factor * (weight_params / running_totals - positive_hot.astype(jnp.float32))
    ).astype(jnp.bfloat16)
    d_queries = jnp.dot(coef16, passage_rows, preferred_element_type=jnp.float32)
    d_passages = jnp.dot(coef16.T, query_rows, preferred_element_type=jnp.float32)
    joined = jnp.concatenate(
        [
            d_queries.reshape(groups, QDEV, feature_count),
            d_passages.reshape(groups, -1, feature_count),
        ],
        axis=1,
    )
    return (loss, joined)


def on_device(
    hidden, lengths, positives, negatives, in_gain, wq, wkv, q_gain, k_gain, wo, out_gain
):
    tensor_count = lax.axis_size("tensor")
    own_rows = hidden.shape[0]
    tokens_count = own_rows * tensor_count
    head_width = wq.shape[1]
    root = math.sqrt(head_width)
    is_even = lax.axis_index("tensor") % 2 == 0
    own_index = lax.axis_index("tensor") * own_rows + jnp.arange(own_rows, dtype=jnp.int32)
    inside, position, last = segment_layout(lengths[0], tokens_count)
    hidden32 = hidden.astype(jnp.float32)
    inverse_in = rms_scale(hidden32)
    normed = (hidden32 * inverse_in * in_gain).astype(jnp.bfloat16)
    partner = swapped(wkv, "tensor", 0)
    both = jnp.concatenate(
        [jnp.where(is_even, wkv, partner), jnp.where(is_even, partner, wkv)], axis=1
    )
    piece = lax.all_gather(normed, "tensor", axis=0, tiled=True)
    kv_raw = jnp.dot(piece, both, preferred_element_type=jnp.float32)
    key_raw = kv_raw[:, :head_width]
    value_raw = kv_raw[:, head_width:]
    value16 = value_raw.astype(jnp.bfloat16)
    cos_key, sin_key = rope_tables(position, head_width)
    key_unit, key_inverse, key_rot = head_forward(key_raw, k_gain, cos_key, sin_key)
    key16 = key_rot.astype(jnp.bfloat16)
    last_rows = jnp.take(piece, last, axis=0)
    query_raw = jnp.dot(last_rows, wq, preferred_element_type=jnp.float32)
    cos_query, sin_query = rope_tables(jnp.take(position, last), head_width)
    query_unit, query_inverse, query_rot = head_forward(query_raw, q_gain, cos_query, sin_query)
    query16 = query_rot.astype(jnp.bfloat16)
    shift = root * jnp.max(q_gain) * jnp.max(k_gain)
    scores = jnp.dot(query16, key16.T, preferred_element_type=jnp.float32) / root
    weight_params = jnp.where(inside.T, jnp.exp(scores - shift), 0.0)
    probs = weight_params / jnp.sum(weight_params, axis=-1, keepdims=True)
    probs16 = probs.astype(jnp.bfloat16)
    attn16 = jnp.dot(probs16, value16, preferred_element_type=jnp.float32).astype(jnp.bfloat16)
    own_last = (last[:, None] == own_index[None, :]).astype(jnp.float32)
    partial_rows = jnp.dot(attn16, wo, preferred_element_type=jnp.float32)
    partial_rows = partial_rows + jnp.dot(own_last, hidden32, precision=lax.Precision.HIGHEST)
    resid = lax.psum(partial_rows, "tensor")
    resid_inverse = rms_scale(resid)
    resid_unit = resid * resid_inverse
    final = resid_unit * out_gain
    final_inverse = lax.rsqrt(jnp.sum(final * final, axis=-1, keepdims=True) + EPSILON)
    embed = final * final_inverse
    everyone = lax.all_gather(embed.astype(jnp.bfloat16), "dp", axis=0, tiled=True)
    groups = lax.axis_size("dp")
    loss, d_every = contrast(everyone.reshape(groups, -1, everyone.shape[1]), positives, negatives)
    d_embed = lax.dynamic_index_in_dim(d_every, lax.axis_index("dp"), 0, keepdims=False)
    d_final = final_inverse * (d_embed - embed * jnp.sum(embed * d_embed, axis=-1, keepdims=True))
    d_resid = norm_backward(d_final, resid_unit, resid_inverse, out_gain)
    d_attn16 = jnp.dot(
        d_resid.astype(jnp.bfloat16), wo.T, preferred_element_type=jnp.float32
    ).astype(jnp.bfloat16)
    d_probs = jnp.dot(d_attn16, value16.T, preferred_element_type=jnp.float32)
    d_scores16 = (
        probs * (d_probs - jnp.sum(probs * d_probs, axis=-1, keepdims=True)) / root
    ).astype(jnp.bfloat16)
    d_query_rot = jnp.dot(d_scores16, key16, preferred_element_type=jnp.float32)
    d_key_rot = jnp.dot(d_scores16.T, query16, preferred_element_type=jnp.float32)
    d_value = jnp.dot(probs16.T, d_attn16, preferred_element_type=jnp.float32)
    d_key_raw = head_backward(d_key_rot, key_unit, key_inverse, k_gain, cos_key, sin_key)
    d_query_raw = head_backward(
        d_query_rot, query_unit, query_inverse, q_gain, cos_query, sin_query
    )
    mine = jnp.where(is_even, d_key_raw, d_value)
    theirs = jnp.where(is_even, d_value, d_key_raw)
    column16 = (mine + swapped(theirs, "tensor", 0)).astype(jnp.bfloat16)
    query_term = jnp.dot(d_query_raw.astype(jnp.bfloat16), wq.T, preferred_element_type=jnp.float32)
    row_index = jnp.arange(own_rows * lax.axis_size("tensor"), dtype=jnp.int32)
    chosen = (row_index[:, None] == last[None, :]).astype(jnp.float32)
    product = jnp.dot(column16, wkv.T, preferred_element_type=jnp.float32)
    d_normed = lax.psum_scatter(
        (product + jnp.dot(chosen, query_term, precision=lax.Precision.HIGHEST)).astype(
            jnp.bfloat16
        ),
        "tensor",
        scatter_dimension=0,
        tiled=True,
    ).astype(jnp.float32)
    d_hidden = norm_backward(d_normed, hidden32 * inverse_in, inverse_in, in_gain)
    d_hidden = d_hidden + jnp.dot(own_last.T, d_resid, precision=lax.Precision.HIGHEST)
    return (d_hidden.astype(jnp.bfloat16), loss)


def solution(mesh):
    placed = (
        P(("dp", "tensor"), None),
        P("dp", None),
        P(),
        P(),
        P(),
        P(None, "tensor"),
        P(None, "tensor"),
        P(),
        P(),
        P("tensor", None),
        P(),
    )
    return jax.shard_map(
        on_device,
        mesh=mesh,
        in_specs=placed,
        out_specs=(P(("dp", "tensor"), None), P()),
        check_vma=False,
    )
```

profile of v0, /device:TPU:0, one launch (start us, length us, event | category | flops | bytes accessed | tf_op | source)
XLA Modules:
  0.0 210.8 jit_solution(16112346342537172633)
XLA Ops:
  7.3 1.4 fusion.16
  8.7 2.0 fusion.12
  10.8 3.0 %collective-permute-start = (bf16[4096,128]{1,0:T(8,128)(2,1)S(1)}, bf16[4096,128]{1,0:T(8,128)(2,1)}, u32[]{:S(2)}, u32[]{:S(2)}) collective-permute-start(bf16[4096,128]{1,0:T(8,128)(2,1)S(1)} %copy-done.3), channel_id=1, source_target_pairs={{0,1},{1,0},{2,3},{3,2},{4,5},{5,4},{6,7},{7,6},{8,9},{9,8},{10,11... | collective-permute-start | bytes 3145736 | tf_op jit(solution)/shard_map/ppermute | solution.py:20
  14.3 0.7 reduce_max.19
  15.0 0.6 reduce_max.18
  16.9 0.7 gather_fusion.1
  18.0 26.0 %collective-permute-done = bf16[4096,128]{1,0:T(8,128)(2,1)} collective-permute-done((bf16[4096,128]{1,0:T(8,128)(2,1)S(1)}, bf16[4096,128]{1,0:T(8,128)(2,1)}, u32[]{:S(2)}, u32[]{:S(2)}) %collective-permute-start) | collective-permute-done | bytes 1048608 | tf_op jit(solution)/shard_map/ppermute | solution.py:20
  44.0 2.7 %broadcast_select_fusion.1 = (bf16[4096,128]{1,0:T(8,128)(2,1)}, bf16[4096,128]{1,0:T(8,128)(2,1)}) fusion(bf16[4096,128]{1,0:T(8,128)(2,1)S(1)} %copy-done.3, bf16[4096,128]{1,0:T(8,128)(2,1)} %collective-permute-done, pred[]{:T(512)S(6)} %eq.62), kind=kLoop, calls=%fused_computation.32 | loop fusion | flops 1048576 | bytes 4194305 | tf_op jit(solution)/shard_map/jit(_where)/select_n | solution.py:117
  46.8 7.6 %all-gather.3.cloned.1.call-done = bf16[256,4096]{1,0:T(8,128)(2,1)} async-done(((bf16[64,4096]{1,0:T(8,128)(2,1)}), bf16[256,4096]{1,0:T(8,128)(2,1)}) %all-gather.3.cloned.1.call-update) | async-done | bytes 2097168 | tf_op jit(solution)/shard_map/all_gather | solution.py:119
  54.4 2.8 %gather_fusion = bf16[32,4096]{1,0:T(8,128)(2,1)S(1)} fusion(bf16[256,4096]{1,0:T(8,128)(2,1)} %all-gather.3.cloned.1.call-done, s32[1024]{0:T(1024)S(1)} %pad_clamp_fusion), kind=kCustom, calls=%fused_computation | custom fusion | bytes 524416 | tf_op jit(solution)/shard_map/jit(_take)/gather | solution.py:127
  57.9 3.2 %fusion.2 = f32[256,256]{0,1:T(8,128)S(1)} fusion(bf16[256,4096]{1,0:T(8,128)(2,1)} %all-gather.3.cloned.1.call-done, bf16[4096,128]{1,0:T(8,128)(2,1)} %get-tuple-element.15, bf16[4096,128]{1,0:T(8,128)(2,1)} %get-tuple-element.14), kind=kOutput, calls=%fused_computation.9 | convolution fusion | flops 541065216 | bytes 4456448 | tf_op jit(solution)/shard_map/dot_general | solution.py:120
  62.2 0.6 copy-done.9
  62.8 0.7 fusion.88
  63.6 1.8 convolution_add_fusion.2
  65.5 46.7 %all-reduce.2.cloned.1.call-done = f32[32,4096]{1,0:T(8,128)} async-done(((f32[32,4096]{1,0:T(8,128)}), f32[32,4096]{1,0:T(8,128)}) %all-reduce.2.cloned.1.call-update) | async-done | bytes 524304 | tf_op jit(solution)/shard_map/psum | solution.py:141
  112.2 1.2 multiply_reduce_fusion.3
  113.4 1.3 multiply_reduce_fusion.2
  114.7 1.9 fusion.25
  117.1 28.8 %all-gather.5.cloned.1.call-done = bf16[256,4096]{1,0:T(8,128)(2,1)} async-done(((bf16[32,4096]{1,0:T(8,128)(2,1)}), bf16[256,4096]{1,0:T(8,128)(2,1)}) %all-gather.5.cloned.1.call-update) | async-done | bytes 2097168 | tf_op jit(solution)/shard_map/all_gather | solution.py:147
  145.8 1.5 slice.60
  147.4 1.8 select_reduce_fusion
  149.3 1.4 fusion.52
  150.8 1.7 fusion.19
  153.2 0.5 copy-done.6
  156.1 1.5 collective-permute-start.1
  158.2 1.8 fusion.42
  160.0 1.9 collective-permute-done.1
  161.8 2.1 %fusion = bf16[256,4096]{1,0:T(8,128)(2,1)} fusion(f32[256,4096]{1,0:T(8,128)S(1)} %fusion.42, bf16[4096,128]{1,0:T(8,128)(2,1)S(1)} %copy-done.4, f32[256,128]{0,1:T(8,128)S(1)} %collective-permute-done.1, f32[256,128]{0,1:T(8,128)S(1)} %get-tuple-element.32, pred[]{:T(512)S(6)} %eq.62, f32[256,128]{0,1:T(8,128)S(1)} %get-tuple-element.7, ...), kind=kOutput, calls=%fused_computation.3 | convolution fusion | flops 270761984 | bytes 7866369 | tf_op jit(solution)/shard_map/dot_general | solution.py:173
  164.0 0.6 subtract_reduce_fusion
  165.2 33.6 %reduce-scatter.2.cloned.1.call-done = bf16[64,4096]{1,0:T(8,128)(2,1)} async-done(((bf16[256,4096]{1,0:T(8,128)(2,1)}), bf16[64,4096]{1,0:T(8,128)(2,1)}) %reduce-scatter.2.cloned.1.call-update) | async-done | bytes 524304 | tf_op jit(solution)/shard_map/reduce_scatter | solution.py:174
  198.8 1.4 fusion.13
  200.2 2.9 %fusion.1 = bf16[64,4096]{1,0:T(8,128)(2,1)} fusion(bf16[64,4096]{1,0:T(8,128)(2,1)S(1)} %copy-done.2, bf16[64,4096]{1,0:T(8,128)(2,1)} %reduce-scatter.2.cloned.1.call-done, f32[64]{0:T(128)S(1)} %broadcast_multiply_fusion.5, f32[4096]{0:T(1024)S(1)} %copy-done.11, f32[64]{0:T(128)S(1)} %copy-done.30, s32[64]{0:T(128)S(1)} %copy-done.34, ...), kind=kOutput, calls=%fused_computation.5 | convolution fusion | flops 104335360 | bytes 2655616 | tf_op jit(solution)/shard_map/dot_general | solution.py:183
  (130 shorter events, 6.9 us)
Async XLA Ops:
  7.2 50.1 %copy-start = (bf16[4096,128]{1,0:T(8,128)(2,1)S(1)}, bf16[4096,128]{1,0:T(8,128)(2,1)}, u32[]{:S(2)}) copy-start(bf16[4096,128]{1,0:T(8,128)(2,1)} %param.16) | copy-start | bytes 3145732
  7.2 10.6 %copy-start.2 = (bf16[64,4096]{1,0:T(8,128)(2,1)S(1)}, bf16[64,4096]{1,0:T(8,128)(2,1)}, u32[]{:S(2)}) copy-start(bf16[64,4096]{1,0:T(8,128)(2,1)} %param.11) | copy-start | bytes 1572868
  7.2 3.6 %copy-start.3 = (bf16[4096,128]{1,0:T(8,128)(2,1)S(1)}, bf16[4096,128]{1,0:T(8,128)(2,1)}, u32[]{:S(2)}) copy-start(bf16[4096,128]{1,0:T(8,128)(2,1)} %param.17) | copy-start | bytes 3145732
  7.2 6.6 %copy-start.35 = (s32[1,32]{1,0:T(1,128)S(1)}, s32[1,32]{1,0:T(1,128)}, u32[]{:S(2)}) copy-start(s32[1,32]{1,0:T(1,128)} %param.12) | copy-start | bytes 388
  7.2 7.1 %copy-start.24 = (f32[128]{0:T(128)S(1)}, f32[128]{0:T(128)}, u32[]{:S(2)}) copy-start(f32[128]{0:T(128)} %param.19) | copy-start | bytes 1540
  7.2 7.7 %copy-start.19 = (f32[128]{0:T(128)S(1)}, f32[128]{0:T(128)}, u32[]{:S(2)}) copy-start(f32[128]{0:T(128)} %param.18) | copy-start | bytes 1540
  7.2 47.2 %all-gather.3.cloned.1.call-start = ((), (), s32[]{:S(2)}) async-start(), calls=%async_computation.1 | async-start | bytes 2621440 | tf_op jit(solution)/shard_map/all_gather | solution.py:119
  8.7 38.1 %copy-start.29 = (f32[64]{0:T(128)}, f32[64]{0:T(128)S(1)}, u32[]{:S(2)}) copy-start(f32[64]{0:T(128)S(1)} %add_rsqrt_fusion.4) | copy-start | bytes 772
  10.8 101.4 %all-reduce.2.cloned.1.call-start = ((), (), s32[]{:S(2)}) async-start(), calls=%async_computation.2 | async-start | bytes 1048576 | tf_op jit(solution)/shard_map/psum | solution.py:141
  10.8 33.2 %collective-permute-start = (bf16[4096,128]{1,0:T(8,128)(2,1)S(1)}, bf16[4096,128]{1,0:T(8,128)(2,1)}, u32[]{:S(2)}, u32[]{:S(2)}) collective-permute-start(bf16[4096,128]{1,0:T(8,128)(2,1)S(1)} %copy-done.3), channel_id=1, source_target_pairs={{0,1},{1,0},{2,3},{3,2},{4,5},{5,4},{6,7},{7,6},{8,9},{9,8},{10,11... | collective-permute-start | bytes 3145736 | tf_op jit(solution)/shard_map/ppermute | solution.py:20
  14.1 32.7 %copy-start.22 = (s32[32]{0:T(128)}, s32[32]{0:T(128)S(1)}, u32[]{:S(2)}) copy-start(s32[32]{0:T(128)S(1)} %get-tuple-element.5) | copy-start | bytes 388
  14.1 3.4 %copy-start.36 = (s32[32]{0:T(128)}, s32[32]{0:T(128)S(1)}, u32[]{:S(2)}) copy-start(s32[32]{0:T(128)S(1)} %fusion.80) | copy-start | bytes 388
  14.2 32.6 %copy-start.31 = (s32[32]{0:T(128)}, s32[32]{0:T(128)S(1)}, u32[]{:S(2)}) copy-start(s32[32]{0:T(128)S(1)} %broadcast_add_fusion) | copy-start | bytes 388
  17.6 29.2 %copy-start.33 = (s32[64]{0:T(128)}, s32[64]{0:T(128)S(1)}, u32[]{:S(2)}) copy-start(s32[64]{0:T(128)S(1)} %iota_add_fusion) | copy-start | bytes 772
  57.7 3.6 %copy-start.16 = (f32[32]{0:T(128)}, f32[32]{0:T(128)S(1)}, u32[]{:S(2)}) copy-start(f32[32]{0:T(128)S(1)} %add_rsqrt_fusion.3) | copy-start | bytes 388
  57.9 3.4 %copy-start.20 = (f32[128]{0:T(128)S(1)}, f32[128]{0:T(128)}, u32[]{:S(2)}) copy-start(f32[128]{0:T(128)} %param.18) | copy-start | bytes 1540
  57.9 3.9 %copy-start.25 = (f32[128]{0:T(128)S(1)}, f32[128]{0:T(128)}, u32[]{:S(2)}) copy-start(f32[128]{0:T(128)} %param.19) | copy-start | bytes 1540
  57.9 5.0 %copy-start.23 = (s32[32]{0:T(128)S(1)}, s32[32]{0:T(128)}, u32[]{:S(2)}) copy-start(s32[32]{0:T(128)} %copy-done.22) | copy-start | bytes 388
  57.9 5.0 %copy-start.37 = (s32[32]{0:T(128)S(1)}, s32[32]{0:T(128)}, u32[]{:S(2)}) copy-start(s32[32]{0:T(128)} %copy-done.36) | copy-start | bytes 388
  57.9 5.7 %copy-start.5 = (bf16[128,4096]{1,0:T(8,128)(2,1)S(1)}, bf16[128,4096]{1,0:T(8,128)(2,1)}, u32[]{:S(2)}) copy-start(bf16[128,4096]{1,0:T(8,128)(2,1)} %param.20) | copy-start | bytes 3145732
  61.2 52.1 %copy-start.8 = (f32[4096]{0:T(1024)S(1)}, f32[4096]{0:T(1024)}, u32[]{:S(2)}) copy-start(f32[4096]{0:T(1024)} %param.21) | copy-start | bytes 49156
  65.4 51.4 %copy-start.27 = (s32[64]{0:T(128)S(1)}, s32[64]{0:T(128)}, u32[]{:S(2)}) copy-start(s32[64]{0:T(128)} %param.13) | copy-start | bytes 772
  65.4 51.5 %copy-start.28 = (s32[64,7]{0,1:T(8,128)S(1)}, s32[64,7]{0,1:T(8,128)}, u32[]{:S(2)}) copy-start(s32[64,7]{0,1:T(8,128)} %param.14) | copy-start | bytes 5380
  65.4 80.4 %all-gather.5.cloned.1.call-start = ((), (), s32[]{:S(2)}) async-start(), calls=%async_computation.3 | async-start | bytes 2359296 | tf_op jit(solution)/shard_map/all_gather | solution.py:147
  116.6 82.2 %reduce-scatter.2.cloned.1.call-start = ((), (), s32[]{:S(2)}) async-start(), calls=%async_computation.4 | async-start | bytes 2621440 | tf_op jit(solution)/shard_map/reduce_scatter | solution.py:174
  152.9 2.5 %copy-start.13 = (f32[256]{0:T(256)S(1)}, f32[256]{0:T(256)}, u32[]{:S(2)}) copy-start(f32[256]{0:T(256)} %copy-done.12) | copy-start | bytes 3076
  154.3 3.9 %copy-start.32 = (s32[32]{0:T(128)S(1)}, s32[32]{0:T(128)}, u32[]{:S(2)}) copy-start(s32[32]{0:T(128)} %copy-done.31) | copy-start | bytes 388
  156.1 5.7 %collective-permute-start.1 = (f32[256,128]{0,1:T(8,128)S(1)}, f32[256,128]{0,1:T(8,128)S(1)}, u32[]{:S(2)}, u32[]{:S(2)}) collective-permute-start(f32[256,128]{0,1:T(8,128)S(1)} %get-tuple-element.31), channel_id=1, source_target_pairs={{0,1},{1,0},{2,3},{3,2},{4,5},{5,4},{6,7},{7,6},{8,9},{9,8},{10,11... | collective-permute-start | bytes 393224 | tf_op jit(solution)/shard_map/ppermute | solution.py:20
  158.1 3.7 %copy-start.4 = (bf16[4096,128]{1,0:T(8,128)(2,1)S(1)}, bf16[4096,128]{1,0:T(8,128)(2,1)}, u32[]{:S(2)}) copy-start(bf16[4096,128]{1,0:T(8,128)(2,1)} %param.17) | copy-start | bytes 3145732
  163.9 34.9 %copy-start.11 = (f32[4096]{0:T(1024)S(1)}, f32[4096]{0:T(1024)}, u32[]{:S(2)}) copy-start(f32[4096]{0:T(1024)} %param.15) | copy-start | bytes 49156
  164.0 34.9 %copy-start.30 = (f32[64]{0:T(128)S(1)}, f32[64]{0:T(128)}, u32[]{:S(2)}) copy-start(f32[64]{0:T(128)} %copy-done.29) | copy-start | bytes 772
  164.0 36.3 %copy-start.34 = (s32[64]{0:T(128)S(1)}, s32[64]{0:T(128)}, u32[]{:S(2)}) copy-start(s32[64]{0:T(128)} %copy-done.33) | copy-start | bytes 772
  (12 other events, 20.2 us)
Sparse Core Ops, SparseCore 0:
  10.9 43.4 all-gather.2
  65.6 46.5 all-reduce.1
  116.7 29.0 all-gather.4
  164.1 34.6 reduce-scatter.1
where the time goes:
time: 211 us
  waiting for transfers between devices  145 us (69%)
  matrix products  20 us (9%)
  between operations  17.4 us (8%)
  other arithmetic  17 us (8%)
  local copies, waits for them, and re-layouts  6.84 us (3%)
  starting transfers between devices  4.88 us (2%)
    psum x1, waiting for transfers between devices, on_device(): resid = lax.psum(partial_rows, 'tensor')  46.7 us
    reduce_scatter x1, waiting for transfers between devices, on_device(): lax.psum_scatter((product + jnp.dot(chosen, query_term, precision=lax.Pre...  33.6 us
    all_gather x1, waiting for transfers between devices, on_device(): lax.all_gather(embed.astype(jnp.bfloat16), 'dp', axis=0, tiled=True)  28.8 us
    ppermute x2, waiting for transfers between devices, swapped(): return lax.ppermute(value, axis, pairs)  27.9 us
    all_gather x1, waiting for transfers between devices, on_device(): piece = lax.all_gather(normed, 'tensor', axis=0, tiled=True)  7.62 us
    ppermute x2, starting transfers between devices, swapped(): return lax.ppermute(value, axis, pairs)  4.53 us
  transfers between devices with their start and end apart: 6, of which 6 were waited for; matrix products, arithmetic and copies ran while one was open for 4% of the time, Pallas kernels for 0%

commit v1 on v0

v1 whole, which is shorter than its diff:
```python
import functools
import math

import jax
import jax.numpy as jnp
from jax import lax
from jax.experimental import pallas as pl
from jax.experimental.pallas import tpu as pltpu
from jax.sharding import PartitionSpec as P

QDEV = 8
EPSILON = 1e-06
SOFTMAX_TEMPER = 0.05
LOSS_MULTIPLIER = 8192.0
ROPE_BASE = 1000000.0

F32 = jnp.float32
BF16 = jnp.bfloat16
MESH = pl.DeviceIdType.MESH
EXACT = lax.Precision.HIGHEST


def nn(a, b, precision=None):
    return jnp.dot(a, b, preferred_element_type=F32, precision=precision)


def nt(a, b, precision=None):
    dims = (((1,), (1,)), ((), ()))
    return lax.dot_general(a, b, dims, preferred_element_type=F32, precision=precision)


def iota(shape, axis):
    return lax.broadcasted_iota(jnp.int32, shape, axis)


def onehot(mask, kind=BF16):
    return jnp.where(mask, 1.0, 0.0).astype(F32).astype(kind)


def rms_scale(x):
    return lax.rsqrt(jnp.mean(x * x, axis=-1, keepdims=True) + EPSILON)


def rope_tables(position, width):
    half = width // 2
    lane = iota((1, width), 1)
    lane = jnp.where(lane >= half, lane - half, lane).astype(F32)
    frequency = jnp.exp(lane * (-2.0 / width * math.log(ROPE_BASE)))
    angles = position * frequency
    return jnp.cos(angles), jnp.sin(angles)


def rotate(x, cosine, sine):
    half = x.shape[-1] // 2
    sign = jnp.where(iota((1, x.shape[-1]), 1) < half, -1.0, 1.0)
    return x * cosine + pltpu.roll(x, half, 1) * sign * sine


def head_forward(raw, gain, cosine, sine):
    inverse = rms_scale(raw)
    unit = raw * inverse
    return unit, inverse, rotate(unit * gain, cosine, sine)


def head_backward(grad, unit, inverse, gain, cosine, sine):
    scaled = rotate(grad, cosine, -sine) * gain
    return inverse * (scaled - unit * jnp.mean(unit * scaled, axis=-1, keepdims=True))


def kernel(
    tensors, groups,
    hidden, lens, positives, negatives, in_gain, wq, wkv, q_gain, k_gain, wo, out_gain,
    out, loss,
    hid_own, hid_all, inv_all, normed, wkv_all, wq_all, wo_all,
    kvp_out, kvp_in, qp_out, qp_in, attn_all, sums_all, embeds, logit_all,
    dap_out, dap_in, pair_out, pair_in, dkv_all, dq_all, rows_all, out16,
    local_sem, tsend, trecv, fsend, frecv, zsend, zrecv, psend, precv,
):
    T, G = tensors, groups
    Z = G // 2
    own, D = hidden.shape
    F = D // T
    HD = wq.shape[1]
    N = own * T
    S = lens.shape[1]
    Q = positives.shape[1]
    H = F // 2
    HH = HD // 2
    root = math.sqrt(HD)
    t = lax.axis_index("tensor")
    g = lax.axis_index("dp")
    zz = g // 2
    core = g % 2
    buddy = g + 1 - 2 * core
    mate = t + 1 - 2 * (t % 2)
    even = t % 2 == 0
    peers = [lax.rem(t + k, T) for k in range(1, T)]
    sources = [lax.rem(t + T - k, T) for k in range(1, T)]
    slots = list(range(T))
    columns = pl.ds(pl.multiple_of(t * F, 128), F)

    own_copies = [
        pltpu.make_async_copy(hidden, hid_own, local_sem.at[0]),
        pltpu.make_async_copy(
            hidden.at[:, columns], hid_all.at[pl.ds(t * own, own)], local_sem.at[1]
        ),
        pltpu.make_async_copy(wkv.at[pl.ds(t * F, F)], wkv_all.at[t], local_sem.at[2]),
        pltpu.make_async_copy(wq.at[pl.ds(t * F, F)], wq_all.at[t], local_sem.at[3]),
        pltpu.make_async_copy(wo.at[:, columns], wo_all.at[t], local_sem.at[4]),
    ]
    for copy in own_copies:
        copy.start()

    barrier = pltpu.get_barrier_semaphore()
    for p in peers:
        pl.semaphore_signal(barrier, inc=1, device_id=(g, p), device_id_type=MESH)
    for k in range(1, Z):
        far = lax.rem(zz + k, Z) * 2 + core
        pl.semaphore_signal(barrier, inc=1, device_id=(far, t), device_id_type=MESH)
    pl.semaphore_signal(barrier, inc=1, device_id=(buddy, t), device_id_type=MESH)
    pl.semaphore_wait(barrier, T - 1 + Z - 1 + 1)

    waits = []

    def to_peer(kind, k, src, dst):
        copy = pltpu.make_async_remote_copy(
            src_ref=src, dst_ref=dst, send_sem=tsend.at[kind, k], recv_sem=trecv.at[kind, k],
            device_id=(g, peers[k]), device_id_type=MESH,
        )
        copy.start()
        waits.append(copy)
        return copy

    def to_buddy(kind, k, src, dst):
        copy = pltpu.make_async_remote_copy(
            src_ref=src, dst_ref=dst, send_sem=fsend.at[kind, k], recv_sem=frecv.at[kind, k],
            device_id=(buddy, t), device_id_type=MESH,
        )
        copy.start()
        waits.append(copy)
        return copy

    def landed(copies):
        for copy in copies:
            copy.wait_recv()

    rest = range(T - 1)
    my_rows = pl.ds(pl.multiple_of(t * own, own), own)

    def cols(p):
        return pl.ds(pl.multiple_of(p * F, 128), F)

    hid_copies = [
        to_peer(0, k, hidden.at[:, cols(peers[k])], hid_all.at[my_rows]) for k in rest
    ]

    def half_rows(p):
        return pl.ds(pl.multiple_of(p * F + core * H, H), H)

    my_half = pl.ds(pl.multiple_of(core * H, H), H)
    my_head_half = pl.ds(pl.multiple_of(core * HH, HH), HH)
    wkv_copies = [
        to_peer(1, k, wkv.at[half_rows(peers[k])], wkv_all.at[t, my_half]) for k in rest
    ]

    own_copies[0].wait()
    mine = hid_own[...].astype(F32)
    inv_all[my_rows, :] = jnp.broadcast_to(rms_scale(mine), (own, HD))
    inv_copies = [to_peer(2, k, inv_all.at[my_rows], inv_all.at[my_rows]) for k in rest]

    lens_row = lens[...].astype(F32)
    square_r, square_c = iota((S, S), 0), iota((S, S), 1)
    lens_col = jnp.sum(jnp.where(square_r == square_c, lens_row, 0.0), axis=1, keepdims=True)
    ends_col = jnp.sum(jnp.where(square_c <= square_r, lens_row, 0.0), axis=1, keepdims=True)
    ends_row = jnp.sum(jnp.where(square_r <= square_c, lens_col, 0.0), axis=0, keepdims=True)
    starts_col, starts_row = ends_col - lens_col, ends_row - lens_row
    token_row = iota((S, N), 1).astype(F32)
    token_col = iota((N, S), 0).astype(F32)
    inside = (token_row >= starts_col) & (token_row < ends_col)
    inside_t = (token_col >= starts_row) & (token_col < ends_row)
    offset = jnp.sum(jnp.where(inside_t, starts_row, 0.0), axis=1, keepdims=True)
    position = iota((N, 1), 0).astype(F32) - offset
    last_hot = onehot(token_row == ends_col - 1.0)
    last_hot_t = onehot(token_col == ends_row - 1.0)
    cos_key, sin_key = rope_tables(position, HD)
    cos_query, sin_query = rope_tables(lens_col - 1.0, HD)
    qg, kg = q_gain[...], k_gain[...]
    shift = root * jnp.max(qg, axis=1, keepdims=True) * jnp.max(kg, axis=1, keepdims=True)
    gain = in_gain[:, columns]
    ogain = out_gain[:, columns]

    wkv_fwd = []
    for k in rest:
        wkv_copies[k].wait_recv()
        spot = wkv_all.at[sources[k], my_half]
        wkv_fwd.append(to_buddy(0, k, spot, spot))
    wq_copies = [
        to_peer(3, k, wq.at[half_rows(peers[k])], wq_all.at[t, my_half]) for k in rest
    ]

    own_copies[1].wait()
    landed(hid_copies)
    landed(inv_copies)
    hid32 = hid_all[...].astype(F32)
    normed[...] = (hid32 * inv_all[:, 0:1] * gain).astype(BF16)
    own_copies[2].wait()
    landed(wkv_fwd)
    for b in slots:
        kvp_out[b] = nn(normed[...], wkv_all[b]).astype(BF16)

    def pair(p):
        return pl.ds((p // 2) * 2, 2)

    kvp_copies = [to_peer(4, k, kvp_out.at[pair(peers[k])], kvp_in.at[t]) for k in rest]
    kvp_in[t] = kvp_out[pair(t)]

    wq_fwd = []
    for k in rest:
        wq_copies[k].wait_recv()
        spot = wq_all.at[sources[k], my_half]
        wq_fwd.append(to_buddy(1, k, spot, spot))
    wo_copies = [
        to_peer(
            5, k, wo.at[my_head_half, cols(peers[k])], wo_all.at[t, my_head_half]
        )
        for k in rest
    ]
    last16 = nn(last_hot, normed[...]).astype(BF16)
    hid_last = nn(last_hot, hid_all[...])
    own_copies[3].wait()
    landed(wq_fwd)
    for b in slots:
        qp_out[b] = nn(last16, wq_all[b])
    qp_copies = [to_peer(6, k, qp_out.at[peers[k]], qp_in.at[t]) for k in rest]
    qp_in[t] = qp_out[t]

    landed(kvp_copies)
    key_raw = kvp_in[0, 0].astype(F32)
    value_raw = kvp_in[0, 1].astype(F32)
    for s in slots[1:]:
        key_raw = key_raw + kvp_in[s, 0].astype(F32)
        value_raw = value_raw + kvp_in[s, 1].astype(F32)
    value16 = value_raw.astype(BF16)
    key_unit, key_inverse, key_rot = head_forward(key_raw, kg, cos_key, sin_key)
    key16 = key_rot.astype(BF16)

    landed(qp_copies)
    query_raw = qp_in[0]
    for s in slots[1:]:
        query_raw = query_raw + qp_in[s]
    query_unit, query_inverse, query_rot = head_forward(query_raw, qg, cos_query, sin_query)
    query16 = query_rot.astype(BF16)
    scores = nt(query16, key16) / root
    weight = jnp.where(inside, jnp.exp(scores - shift), 0.0)
    probs = weight / jnp.sum(weight, axis=-1, keepdims=True)
    probs16 = probs.astype(BF16)
    attn_all[t] = nn(probs16, value16).astype(BF16)
    attn_copies = [to_peer(7, k, attn_all.at[t], attn_all.at[t]) for k in rest]

    wo_fwd = []
    for k in rest:
        wo_copies[k].wait_recv()
        spot = wo_all.at[sources[k], my_head_half]
        wo_fwd.append(to_buddy(2, k, spot, spot))
    own_copies[4].wait()
    landed(wo_fwd)
    landed(attn_copies)

    resid = hid_last
    for s in slots:
        resid = resid + nn(attn_all[s], wo_all[s])
    scaled = resid * ogain
    lane = iota((S, HD), 1)
    sums_all[t] = jnp.where(
        lane == 0,
        jnp.sum(resid * resid, axis=1, keepdims=True),
        jnp.sum(scaled * scaled, axis=1, keepdims=True),
    )
    sums_copies = [to_peer(8, k, sums_all.at[t], sums_all.at[t]) for k in rest]
    landed(sums_copies)
    sums = sums_all[0]
    for s in slots[1:]:
        sums = sums + sums_all[s]
    resid_inverse = lax.rsqrt(sums[:, 0:1] / D + EPSILON)
    final_inverse = lax.rsqrt(resid_inverse * resid_inverse * sums[:, 1:2] + EPSILON)
    resid_unit = resid * resid_inverse
    embed = resid_unit * ogain * final_inverse

    my_seqs = pl.ds(pl.multiple_of(g * S, S), S)
    embeds[my_seqs, :] = embed.astype(BF16)
    z_copies = []
    for k in range(1, Z):
        far = lax.rem(zz + k, Z) * 2 + core
        copy = pltpu.make_async_remote_copy(
            src_ref=embeds.at[my_seqs], dst_ref=embeds.at[my_seqs],
            send_sem=zsend.at[k - 1], recv_sem=zrecv.at[k - 1],
            device_id=(far, t), device_id_type=MESH,
        )
        copy.start()
        waits.append(copy)
        z_copies.append(copy)

    def chip_copy(index, spot):
        copy = pltpu.make_async_remote_copy(
            src_ref=spot, dst_ref=spot, send_sem=psend.at[index], recv_sem=precv.at[index],
            device_id=(buddy, t), device_id_type=MESH,
        )
        copy.start()
        waits.append(copy)
        return copy

    shared = [chip_copy(0, embeds.at[my_seqs])]

    E = G * S
    seq_of = iota((1, E), 1) % S
    passage = jnp.where(seq_of >= QDEV, (iota((1, E), 1) // S) * (S - QDEV) + seq_of - QDEV, -1)
    eye_q = iota((Q, Q), 0) == iota((Q, Q), 1)
    pos_col = jnp.sum(
        jnp.where(eye_q, positives[...].astype(F32), 0.0), axis=1, keepdims=True
    ).astype(jnp.int32)
    pos_hot = pos_col == passage
    neg = negatives[...]
    hard = neg[:, 0:1] == passage
    for j in range(1, neg.shape[1]):
        hard = hard | (neg[:, j : j + 1] == passage)
    positive_f = jnp.where(pos_hot, 1.0, 0.0)
    allowed = (jnp.max(positive_f, axis=0, keepdims=True) > 0.5) | hard
    q_id = iota((Q, E), 0)
    pick_q = onehot(iota((Q, E), 1) == (q_id // QDEV) * S + q_id % QDEV)
    row_s = iota((S, Q), 0)
    own_q = (row_s < QDEV) & (iota((S, Q), 1) == g * QDEV + row_s)
    own_p = iota((S, E), 1) == g * S + iota((S, E), 0)

    for k in range(1, Z):
        z_copies[k - 1].wait_recv()
        origin = lax.rem(zz + Z - k, Z) * 2 + core
        shared.append(chip_copy(k, embeds.at[pl.ds(pl.multiple_of(origin * S, S), S)]))
    landed(shared)

    queries = nn(pick_q, embeds[...]).astype(BF16)
    logit_all[t] = nt(queries, embeds[...])
    logit_copies = [to_peer(9, k, logit_all.at[t], logit_all.at[t]) for k in rest]
    landed(logit_copies)
    dots = logit_all[0]
    for s in slots[1:]:
        dots = dots + logit_all[s]
    logits = dots / SOFTMAX_TEMPER
    grown = jnp.where(allowed, jnp.exp(logits - 1.0 / SOFTMAX_TEMPER), 0.0)
    totals = jnp.sum(grown, axis=1, keepdims=True)
    target = jnp.sum(jnp.where(pos_hot, logits, 0.0), axis=1, keepdims=True)
    each = jnp.log(totals) + 1.0 / SOFTMAX_TEMPER - target
    loss[...] = jnp.broadcast_to(jnp.sum(each, axis=0, keepdims=True) / Q, loss.shape)
    factor = LOSS_MULTIPLIER / (Q * SOFTMAX_TEMPER)
    coef16 = (factor * (grown / totals - positive_f)).astype(BF16)
    along = coef16.astype(F32) * dots
    own_q16, own_p16 = onehot(own_q), onehot(own_p)
    coef_q = nn(own_q16, coef16).astype(BF16)
    coef_p = nt(own_p16, coef16).astype(BF16)
    d_embed = nn(coef_q, embeds[...]) + nn(coef_p, queries)
    inner = jnp.sum(nn(onehot(own_q, F32), along, EXACT), axis=1, keepdims=True) + jnp.sum(
        nt(onehot(own_p, F32), along, EXACT), axis=1, keepdims=True
    )
    d_final = final_inverse * (d_embed - embed * inner)
    middle = inner * (EPSILON / D) * final_inverse * final_inverse
    d_resid = resid_inverse * (ogain * d_final - resid_unit * middle)
    d_resid16 = d_resid.astype(BF16)
    d_resid_low = (d_resid - d_resid16.astype(F32)).astype(BF16)

    for b in slots:
        dap_out[b] = nt(d_resid16, wo_all[b])
    dap_copies = [to_peer(10, k, dap_out.at[peers[k]], dap_in.at[t]) for k in rest]
    dap_in[t] = dap_out[t]
    eye_n = iota((N, N), 0) == iota((N, N), 1)
    eye16 = onehot(eye_n)
    probs16_t = nt(eye16, probs16).astype(BF16)
    landed(dap_copies)
    d_attn = dap_in[0]
    for s in slots[1:]:
        d_attn = d_attn + dap_in[s]
    d_attn16 = d_attn.astype(BF16)
    d_probs = nt(d_attn16, value16)
    d_scores16 = (
        probs * (d_probs - jnp.sum(probs * d_probs, axis=-1, keepdims=True)) / root
    ).astype(BF16)
    d_key_rot = nn(nt(eye16, d_scores16).astype(BF16), query16)
    d_value = nn(probs16_t, d_attn16)
    pair_out[...] = jnp.where(even, d_value, d_key_rot).astype(BF16)
    pair_copy = pltpu.make_async_remote_copy(
        src_ref=pair_out, dst_ref=pair_in, send_sem=psend.at[Z], recv_sem=precv.at[Z],
        device_id=(g, mate), device_id_type=MESH,
    )
    pair_copy.start()
    waits.append(pair_copy)
    d_query_rot = nn(d_scores16, key16)
    d_query16 = head_backward(
        d_query_rot, query_unit, query_inverse, qg, cos_query, sin_query
    ).astype(BF16)
    dq_all[t] = d_query16
    dq_copies = [to_peer(11, k, dq_all.at[t], dq_all.at[t]) for k in rest]
    query_rows = nn(
        last_hot_t.astype(F32), d_query16.astype(F32) * query_raw, EXACT
    )
    pair_copy.wait_recv()
    whole = jnp.where(even, d_key_rot, d_value) + pair_in[...].astype(F32)
    d_key_raw = head_backward(whole, key_unit, key_inverse, kg, cos_key, sin_key)
    column16 = jnp.where(even, d_key_raw, whole).astype(BF16)
    dkv_all[t] = column16
    dkv_copies = [to_peer(12, k, dkv_all.at[t], dkv_all.at[t]) for k in rest]
    raw = jnp.where(even, key_raw, value_raw)
    rows_all[t] = nt(
        jnp.ones((8, HD), F32), column16.astype(F32) * raw + query_rows, EXACT
    )
    row_copies = [to_peer(13, k, rows_all.at[t], rows_all.at[t]) for k in rest]
    landed(dq_copies)
    landed(dkv_copies)
    landed(row_copies)

    row_sums = rows_all[0]
    for s in slots[1:]:
        row_sums = row_sums + rows_all[s]
    out_copies = []
    for k, p in list(enumerate(peers)) + [(None, t)]:
        rows = pl.ds(pl.multiple_of(p * own, own), own)
        hit = iota((own, N), 1) == p * own + iota((own, N), 0)
        mean = jnp.sum(jnp.where(hit, row_sums[0:1, :], 0.0), axis=1, keepdims=True) / D
        last_here = onehot(
            (iota((own, S), 0) + p * own).astype(F32) == ends_row - 1.0
        )
        d_normed = nt(dkv_all[0, rows], wkv_all[0])
        for b in slots:
            if b > 0:
                d_normed = d_normed + nt(dkv_all[b, rows], wkv_all[b])
            d_normed = d_normed + nt(nn(last_here, dq_all[b]).astype(BF16), wq_all[b])
        inverse = inv_all[rows, 0:1]
        unit = hid_all[rows, :].astype(F32) * inverse
        grad = inverse * (d_normed * gain - unit * mean)
        grad = grad + nn(last_here, d_resid16) + nn(last_here, d_resid_low)
        out16[rows, :] = grad.astype(BF16)
        if k is None:
            local = pltpu.make_async_copy(out16.at[rows], out.at[:, columns], local_sem.at[5])
            local.start()
        else:
            out_copies.append(to_peer(14, k, out16.at[rows], out.at[:, columns]))
    landed(out_copies)
    local.wait()
    for copy in waits:
        copy.wait_send()


def on_device(
    tensors, groups,
    hidden, lengths, positives, negatives, in_gain, wq, wkv, q_gain, k_gain, wo, out_gain
):
    T, G = tensors, groups
    own, D = hidden.shape
    F = D // T
    HD = wq.shape[1]
    N = own * T
    S = lengths.shape[1]
    Q = positives.shape[0]
    Z = G // 2
    vmem = pl.BlockSpec(memory_space=pltpu.VMEM)
    anywhere = pl.BlockSpec(memory_space=pl.ANY)
    scratch = [
        pltpu.VMEM((own, D), BF16),
        pltpu.VMEM((N, F), BF16),
        pltpu.VMEM((N, HD), F32),
        pltpu.VMEM((N, F), BF16),
        pltpu.VMEM((T, F, HD), BF16),
        pltpu.VMEM((T, F, HD), BF16),
        pltpu.VMEM((T, HD, F), BF16),
        pltpu.VMEM((T, N, HD), BF16),
        pltpu.VMEM((T, 2, N, HD), BF16),
        pltpu.VMEM((T, S, HD), F32),
        pltpu.VMEM((T, S, HD), F32),
        pltpu.VMEM((T, S, HD), BF16),
        pltpu.VMEM((T, S, HD), F32),
        pltpu.VMEM((G * S, F), BF16),
        pltpu.VMEM((T, Q, G * S), F32),
        pltpu.VMEM((T, S, HD), F32),
        pltpu.VMEM((T, S, HD), F32),
        pltpu.VMEM((N, HD), BF16),
        pltpu.VMEM((N, HD), BF16),
        pltpu.VMEM((T, N, HD), BF16),
        pltpu.VMEM((T, S, HD), BF16),
        pltpu.VMEM((T, 8, N), F32),
        pltpu.VMEM((N, F), BF16),
        pltpu.SemaphoreType.DMA((6,)),
        pltpu.SemaphoreType.DMA((15, T - 1)),
        pltpu.SemaphoreType.DMA((15, T - 1)),
        pltpu.SemaphoreType.DMA((3, T - 1)),
        pltpu.SemaphoreType.DMA((3, T - 1)),
        pltpu.SemaphoreType.DMA((Z - 1,)),
        pltpu.SemaphoreType.DMA((Z - 1,)),
        pltpu.SemaphoreType.DMA((Z + 1,)),
        pltpu.SemaphoreType.DMA((Z + 1,)),
    ]
    d_hidden, loss = pl.pallas_call(
        functools.partial(kernel, T, G),
        out_shape=(
            jax.ShapeDtypeStruct((own, D), BF16),
            jax.ShapeDtypeStruct((8, 128), F32),
        ),
        in_specs=[
            anywhere, vmem, vmem, vmem, vmem, anywhere, anywhere, vmem, vmem, anywhere, vmem
        ],
        out_specs=(anywhere, vmem),
        scratch_shapes=scratch,
        compiler_params=pltpu.CompilerParams(
            collective_id=0, has_side_effects=True, vmem_limit_bytes=48 * 1024 * 1024
        ),
    )(
        hidden, lengths, positives.reshape(1, Q), negatives, in_gain.reshape(1, D), wq, wkv,
        q_gain.reshape(1, HD), k_gain.reshape(1, HD), wo, out_gain.reshape(1, D),
    )
    return d_hidden, loss[0, 0]


def solution(mesh):
    placed = (
        P(("dp", "tensor"), None),
        P("dp", None),
        P(),
        P(),
        P(),
        P(None, "tensor"),
        P(None, "tensor"),
        P(),
        P(),
        P("tensor", None),
        P(),
    )
    return jax.shard_map(
        functools.partial(on_device, mesh.shape["tensor"], mesh.shape["dp"]),
        mesh=mesh,
        in_specs=placed,
        out_specs=(P(("dp", "tensor"), None), P()),
        check_vma=False,
    )
```

time: 211 us -> 86.9 us (0.41)
  waiting for transfers between devices: 145 us -> 0 us
  Pallas kernels: 0 us -> 78.4 us
  matrix products: 20 us -> 0 us
  other arithmetic: 17 us -> 0 us
  between operations: 17.4 us -> 0.69 us
  starting transfers between devices: 4.88 us -> 0 us
    pallas_call x0 -> x1, Pallas kernels: none -> 78.4 us  [on_device(): pl.pallas_call(functools.partial(kernel, T, G), out_shape=(jax.ShapeDtype...]
    psum x1 -> x0, waiting for transfers between devices: 46.7 us -> none  [on_device(): resid = lax.psum(partial_rows, 'tensor')]
    all_gather x2 -> x0, waiting for transfers between devices: 36.4 us -> none  [the longest x1 28.8 us: on_device(): lax.all_gather(embed.astype(jnp.bfloat16), 'dp', axis=0, tiled=True)]
    reduce_scatter x1 -> x0, waiting for transfers between devices: 33.6 us -> none  [on_device(): lax.psum_scatter((product + jnp.dot(chosen, query_term, precision=lax.Pre...]
    ppermute x2 -> x0, waiting for transfers between devices: 27.9 us -> none  [swapped(): return lax.ppermute(value, axis, pairs)]
    dot_general x17 -> x0, matrix products: 20 us -> none  [the longest x1 3.19 us: on_device(): kv_raw = jnp.dot(piece, both, preferred_element_type=jnp.float32)]
    reduce_sum x11 -> x0, other arithmetic: 7.34 us -> none  [the longest x3 2.61 us: rms_scale(): jnp.mean(tensor * tensor, axis=-1, keepdims=True) + EPSILON]
    unnamed x76 -> x24, local copies, waits for them, and re-layouts: 1.62 us -> 6.9 us
  transfers between devices with their start and end apart: 6 -> 0, of which waited for: 6 -> 0; matrix products, arithmetic and copies ran while one was open for 4% -> 0% of each run, Pallas kernels for 0% -> 0%
where the time goes in v1:
time: 86.9 us; the launch traced here: 86.5 us
  Pallas kernels  78.4 us (90%)
  local copies, waits for them, and re-layouts  7.42 us (9%)
    pallas_call x1, Pallas kernels, on_device(): pl.pallas_call(functools.partial(kernel, T, G), out_shape=(jax.ShapeDtype...  78.4 us
    unnamed x24, local copies, waits for them, and re-layouts  6.9 us

profile of v1, /device:TPU:0, one launch (start us, length us, event | category | flops | bytes accessed | tf_op | source)
XLA Modules:
  0.0 86.5 jit_solution(15999625260761462983)
XLA Ops:
  0.6 0.0 copy-start.10
  0.6 0.7 copy-done.10
  1.3 0.0 copy-start.4
  1.3 0.0 copy-start.5
  1.3 0.0 copy-start.6
  1.3 0.0 copy-start.7
  1.3 0.0 copy-start.8
  1.3 0.0 copy-start.9
  1.4 0.1 copy.13.negatives
  1.4 0.6 copy-done.4
  2.0 0.0 copy-done.5
  2.1 0.0 copy-done.6
  2.1 0.0 copy-done.7
  2.1 0.0 copy-done.8
  2.1 0.0 copy-done.9
  2.1 0.0 copy-start
  2.1 1.2 %copy-done = bf16[4096,128]{1,0:T(8,128)(2,1)S(1)} copy-done((bf16[4096,128]{1,0:T(8,128)(2,1)S(1)}, bf16[4096,128]{1,0:T(8,128)(2,1)}, u32[]{:S(2)}) %copy-start) | copy-done | bytes 1048600
  3.3 0.0 copy-start.1
  3.3 1.2 %copy-done.1 = bf16[4096,128]{1,0:T(8,128)(2,1)S(1)} copy-done((bf16[4096,128]{1,0:T(8,128)(2,1)S(1)}, bf16[4096,128]{1,0:T(8,128)(2,1)}, u32[]{:S(2)}) %copy-start.1) | copy-done | bytes 1048600
  4.5 0.0 copy-start.2
  4.5 1.2 %copy-done.2 = bf16[128,4096]{1,0:T(8,128)(2,1)S(1)} copy-done((bf16[128,4096]{1,0:T(8,128)(2,1)S(1)}, bf16[128,4096]{1,0:T(8,128)(2,1)}, u32[]{:S(2)}) %copy-start.2) | copy-done | bytes 1048600
  5.7 0.0 copy-start.3
  5.7 1.0 %copy-done.3 = bf16[64,4096]{1,0:T(8,128)(2,1)S(1)} copy-done((bf16[64,4096]{1,0:T(8,128)(2,1)S(1)}, bf16[64,4096]{1,0:T(8,128)(2,1)}, u32[]{:S(2)}) %copy-start.3) | copy-done | bytes 524312
  6.8 78.4 %shard_map.122 = (bf16[64,4096]{1,0:T(8,128)(2,1)S(1)}, f32[8,128]{1,0:T(8,128)S(1)}) custom-call(bf16[64,4096]{1,0:T(8,128)(2,1)S(1)} %copy-done.3, s32[1,32]{1,0:T(1,128)S(1)} %copy-done.6, s32[1,64]{1,0:T(1,128)S(1)} %bitcast.8, s32[64,7]{1,0:T(8,128)S(1)} %copy.13.negatives, f32[1,4096]{1,0:T(1,128)S(1)} %bitcast.6, bf16[4096,128]{1,0:T(8,128)(2,1)S(1)} %copy-done, ...), custom_call_target="tpu_custom_call" | custom-call | tf_op jit(solution)/shard_map/pallas_call | solution.py:498
  85.2 0.5 slice.3
  85.7 0.8 copy.15
Async XLA Ops:
  0.6 0.7 copy-start.10
  1.3 0.7 copy-start.4
  1.3 0.7 copy-start.5
  1.3 0.7 copy-start.6
  1.3 0.7 copy-start.7
  1.3 0.7 copy-start.8
  1.3 0.7 copy-start.9
  2.1 1.2 %copy-start = (bf16[4096,128]{1,0:T(8,128)(2,1)S(1)}, bf16[4096,128]{1,0:T(8,128)(2,1)}, u32[]{:S(2)}) copy-start(bf16[4096,128]{1,0:T(8,128)(2,1)} %wq.1) | copy-start | bytes 3145732
  3.3 1.2 %copy-start.1 = (bf16[4096,128]{1,0:T(8,128)(2,1)S(1)}, bf16[4096,128]{1,0:T(8,128)(2,1)}, u32[]{:S(2)}) copy-start(bf16[4096,128]{1,0:T(8,128)(2,1)} %wkv.1) | copy-start | bytes 3145732
  4.5 1.2 %copy-start.2 = (bf16[128,4096]{1,0:T(8,128)(2,1)S(1)}, bf16[128,4096]{1,0:T(8,128)(2,1)}, u32[]{:S(2)}) copy-start(bf16[128,4096]{1,0:T(8,128)(2,1)} %wo.1) | copy-start | bytes 3145732
  5.7 1.0 %copy-start.3 = (bf16[64,4096]{1,0:T(8,128)(2,1)S(1)}, bf16[64,4096]{1,0:T(8,128)(2,1)}, u32[]{:S(2)}) copy-start(bf16[64,4096]{1,0:T(8,128)(2,1)} %hidden.1) | copy-start | bytes 1572868

commit v2 on v1

--- a/solution.py
+++ b/solution.py
@@ -71,8 +71,8 @@
     tensors, groups,
     hidden, lens, positives, negatives, in_gain, wq, wkv, q_gain, k_gain, wo, out_gain,
     out, loss,
-    hid_own, hid_all, inv_all, normed, wkv_all, wq_all, wo_all,
-    kvp_out, kvp_in, qp_out, qp_in, attn_all, sums_all, embeds, logit_all,
+    hid_own, hid_all, inv_rows, inv_all, normed, wkv_all, wq_all, wo_all,
+    kvp_out, kvp_in, qp_out, qp_in, attn_all, embeds, logit_all,
     dap_out, dap_in, pair_out, pair_in, dkv_all, dq_all, rows_all, out16,
     local_sem, tsend, trecv, fsend, frecv, zsend, zrecv, psend, precv,
 ):
@@ -165,8 +165,11 @@
 
     own_copies[0].wait()
     mine = hid_own[...].astype(F32)
-    inv_all[my_rows, :] = jnp.broadcast_to(rms_scale(mine), (own, HD))
-    inv_copies = [to_peer(2, k, inv_all.at[my_rows], inv_all.at[my_rows]) for k in rest]
+    diagonal = iota((own, HD), 0) == iota((own, HD), 1)
+    inv_rows[t] = jnp.broadcast_to(
+        jnp.sum(jnp.where(diagonal, rms_scale(mine), 0.0), axis=0, keepdims=True), (8, HD)
+    )
+    inv_copies = [to_peer(2, k, inv_rows.at[t], inv_rows.at[t]) for k in rest]
 
     lens_row = lens[...].astype(F32)
     square_r, square_c = iota((S, S), 0), iota((S, S), 1)
@@ -201,8 +204,13 @@
     own_copies[1].wait()
     landed(hid_copies)
     landed(inv_copies)
-    hid32 = hid_all[...].astype(F32)
-    normed[...] = (hid32 * inv_all[:, 0:1] * gain).astype(BF16)
+    for s in slots:
+        rows = slice(s * own, (s + 1) * own)
+        inverse = jnp.sum(
+            jnp.where(diagonal, inv_rows[s, 0:1, :], 0.0), axis=1, keepdims=True
+        )
+        inv_all[rows, :] = jnp.broadcast_to(inverse, (own, HD))
+        normed[rows, :] = (hid_all[rows, :].astype(F32) * inverse * gain).astype(BF16)
     own_copies[2].wait()
     landed(wkv_fwd)
     for b in slots:
@@ -269,25 +277,8 @@
     resid = hid_last
     for s in slots:
         resid = resid + nn(attn_all[s], wo_all[s])
-    scaled = resid * ogain
-    lane = iota((S, HD), 1)
-    sums_all[t] = jnp.where(
-        lane == 0,
-        jnp.sum(resid * resid, axis=1, keepdims=True),
-        jnp.sum(scaled * scaled, axis=1, keepdims=True),
-    )
-    sums_copies = [to_peer(8, k, sums_all.at[t], sums_all.at[t]) for k in rest]
-    landed(sums_copies)
-    sums = sums_all[0]
-    for s in slots[1:]:
-        sums = sums + sums_all[s]
-    resid_inverse = lax.rsqrt(sums[:, 0:1] / D + EPSILON)
-    final_inverse = lax.rsqrt(resid_inverse * resid_inverse * sums[:, 1:2] + EPSILON)
-    resid_unit = resid * resid_inverse
-    embed = resid_unit * ogain * final_inverse
-
     my_seqs = pl.ds(pl.multiple_of(g * S, S), S)
-    embeds[my_seqs, :] = embed.astype(BF16)
+    embeds[my_seqs, :] = (resid * ogain).astype(BF16)
     z_copies = []
     for k in range(1, Z):
         far = lax.rem(zz + k, Z) * 2 + core
@@ -315,18 +306,21 @@
     seq_of = iota((1, E), 1) % S
     passage = jnp.where(seq_of >= QDEV, (iota((1, E), 1) // S) * (S - QDEV) + seq_of - QDEV, -1)
     eye_q = iota((Q, Q), 0) == iota((Q, Q), 1)
-    pos_col = jnp.sum(
-        jnp.where(eye_q, positives[...].astype(F32), 0.0), axis=1, keepdims=True
-    ).astype(jnp.int32)
-    pos_hot = pos_col == passage
-    neg = negatives[...]
-    hard = neg[:, 0:1] == passage
-    for j in range(1, neg.shape[1]):
-        hard = hard | (neg[:, j : j + 1] == passage)
+
+    def chosen(row):
+        column = jnp.sum(jnp.where(eye_q, row.astype(F32), 0.0), axis=1, keepdims=True)
+        return column.astype(jnp.int32) == passage
+
+    pos_hot = chosen(positives[...])
+    hard = chosen(negatives[0:1, :])
+    for j in range(1, negatives.shape[0]):
+        hard = hard | chosen(negatives[j : j + 1, :])
     positive_f = jnp.where(pos_hot, 1.0, 0.0)
     allowed = (jnp.max(positive_f, axis=0, keepdims=True) > 0.5) | hard
     q_id = iota((Q, E), 0)
-    pick_q = onehot(iota((Q, E), 1) == (q_id // QDEV) * S + q_id % QDEV)
+    pick = iota((Q, E), 1) == (q_id // QDEV) * S + q_id % QDEV
+    pick_q = onehot(pick)
+    eye_e = iota((E, E), 0) == iota((E, E), 1)
     row_s = iota((S, Q), 0)
     own_q = (row_s < QDEV) & (iota((S, Q), 1) == g * QDEV + row_s)
     own_p = iota((S, E), 1) == g * S + iota((S, E), 0)
@@ -338,27 +332,45 @@
     landed(shared)
 
     queries = nn(pick_q, embeds[...]).astype(BF16)
-    logit_all[t] = nt(queries, embeds[...])
+    plain = (embeds[...].astype(F32) * (1.0 / ogain)).astype(BF16)
+    plain_sq = jnp.sum(jnp.where(eye_e, nt(plain, plain), 0.0), axis=0, keepdims=True)
+    scaled_sq = jnp.sum(
+        jnp.where(eye_e, nt(embeds[...], embeds[...]), 0.0), axis=0, keepdims=True
+    )
+    logit_all[t, 0:Q] = nt(queries, embeds[...])
+    logit_all[t, Q : Q + 8] = jnp.where(iota((8, E), 0) == 0, plain_sq, scaled_sq)
     logit_copies = [to_peer(9, k, logit_all.at[t], logit_all.at[t]) for k in rest]
     landed(logit_copies)
-    dots = logit_all[0]
+    summed = logit_all[0]
     for s in slots[1:]:
-        dots = dots + logit_all[s]
-    logits = dots / SOFTMAX_TEMPER
+        summed = summed + logit_all[s]
+    raw_dots = summed[0:Q]
+    inverse_row = lax.rsqrt(summed[Q : Q + 1] / D + EPSILON)
+    final_row = lax.rsqrt(inverse_row * inverse_row * summed[Q + 1 : Q + 2] + EPSILON)
+    scale_row = inverse_row * final_row
+    scale_q = jnp.sum(jnp.where(pick, scale_row, 0.0), axis=1, keepdims=True)
+    resid_inverse = jnp.sum(jnp.where(own_p, inverse_row, 0.0), axis=1, keepdims=True)
+    final_inverse = jnp.sum(jnp.where(own_p, final_row, 0.0), axis=1, keepdims=True)
+    resid_unit = resid * resid_inverse
+    embed = resid_unit * ogain * final_inverse
+    dots_q, dots_p = raw_dots * scale_q, raw_dots * scale_row
+    logits = dots_q * scale_row / SOFTMAX_TEMPER
     grown = jnp.where(allowed, jnp.exp(logits - 1.0 / SOFTMAX_TEMPER), 0.0)
     totals = jnp.sum(grown, axis=1, keepdims=True)
     target = jnp.sum(jnp.where(pos_hot, logits, 0.0), axis=1, keepdims=True)
     each = jnp.log(totals) + 1.0 / SOFTMAX_TEMPER - target
-    loss[...] = jnp.broadcast_to(jnp.sum(each, axis=0, keepdims=True) / Q, loss.shape)
+    loss[0, 0] = jnp.sum(each) / Q
     factor = LOSS_MULTIPLIER / (Q * SOFTMAX_TEMPER)
-    coef16 = (factor * (grown / totals - positive_f)).astype(BF16)
-    along = coef16.astype(F32) * dots
-    own_q16, own_p16 = onehot(own_q), onehot(own_p)
-    coef_q = nn(own_q16, coef16).astype(BF16)
-    coef_p = nt(own_p16, coef16).astype(BF16)
+    coef = factor * (grown / totals - positive_f)
+    coef_q16 = (coef * scale_row).astype(BF16)
+    coef_p16 = (coef * scale_q).astype(BF16)
+    coef_q = nn(onehot(own_q), coef_q16).astype(BF16)
+    coef_p = nt(onehot(own_p), coef_p16).astype(BF16)
     d_embed = nn(coef_q, embeds[...]) + nn(coef_p, queries)
-    inner = jnp.sum(nn(onehot(own_q, F32), along, EXACT), axis=1, keepdims=True) + jnp.sum(
-        nt(onehot(own_p, F32), along, EXACT), axis=1, keepdims=True
+    along_q = coef_q16.astype(F32) * dots_q
+    along_p = coef_p16.astype(F32) * dots_p
+    inner = jnp.sum(nn(onehot(own_q, F32), along_q, EXACT), axis=1, keepdims=True) + jnp.sum(
+        nt(onehot(own_p, F32), along_p, EXACT), axis=1, keepdims=True
     )
     d_final = final_inverse * (d_embed - embed * inner)
     middle = inner * (EPSILON / D) * final_inverse * final_inverse
@@ -464,6 +476,7 @@
     scratch = [
         pltpu.VMEM((own, D), BF16),
         pltpu.VMEM((N, F), BF16),
+        pltpu.VMEM((T, 8, HD), F32),
         pltpu.VMEM((N, HD), F32),
         pltpu.VMEM((N, F), BF16),
         pltpu.VMEM((T, F, HD), BF16),
@@ -474,9 +487,8 @@
         pltpu.VMEM((T, S, HD), F32),
         pltpu.VMEM((T, S, HD), F32),
         pltpu.VMEM((T, S, HD), BF16),
-        pltpu.VMEM((T, S, HD), F32),
         pltpu.VMEM((G * S, F), BF16),
-        pltpu.VMEM((T, Q, G * S), F32),
+        pltpu.VMEM((T, Q + 8, G * S), F32),
         pltpu.VMEM((T, S, HD), F32),
         pltpu.VMEM((T, S, HD), F32),
         pltpu.VMEM((N, HD), BF16),
@@ -499,21 +511,21 @@
         functools.partial(kernel, T, G),
         out_shape=(
             jax.ShapeDtypeStruct((own, D), BF16),
-            jax.ShapeDtypeStruct((8, 128), F32),
+            jax.ShapeDtypeStruct((1, 1), F32),
         ),
         in_specs=[
             anywhere, vmem, vmem, vmem, vmem, anywhere, anywhere, vmem, vmem, anywhere, vmem
         ],
-        out_specs=(anywhere, vmem),
+        out_specs=(anywhere, pl.BlockSpec(memory_space=pltpu.SMEM)),
         scratch_shapes=scratch,
         compiler_params=pltpu.CompilerParams(
-            collective_id=0, has_side_effects=True, vmem_limit_bytes=48 * 1024 * 1024
+            collective_id=0, has_side_effects=True, vmem_limit_bytes=60 * 1024 * 1024
         ),
     )(
-        hidden, lengths, positives.reshape(1, Q), negatives, in_gain.reshape(1, D), wq, wkv,
+        hidden, lengths, positives.reshape(1, Q), negatives.T, in_gain.reshape(1, D), wq, wkv,
         q_gain.reshape(1, HD), k_gain.reshape(1, HD), wo, out_gain.reshape(1, D),
     )
-    return d_hidden, loss[0, 0]
+    return d_hidden, loss.reshape(())
 
 
 def solution(mesh):

time: 86.9 us -> 82.1 us (0.945)
  local copies, waits for them, and re-layouts: 7.42 us -> 1.87 us
  between operations: 0.69 us -> 2.34 us
    unnamed x24 -> x1, local copies, waits for them, and re-layouts: 6.9 us -> 1.87 us
where the time goes in v2:
time: 82.1 us; the launch traced here: 81.8 us
  Pallas kernels  77.6 us (95%)
  between operations  2.34 us (3%)
  local copies, waits for them, and re-layouts  1.87 us (2%)
    pallas_call x1, Pallas kernels, on_device(): pl.pallas_call(functools.partial(kernel, T, G), out_shape=(jax.ShapeDtype...  77.6 us
    unnamed x1, local copies, waits for them, and re-layouts  1.87 us

profile of v2, /device:TPU:0, one launch (start us, length us, event | category | flops | bytes accessed | tf_op | source)
XLA Modules:
  0.0 81.8 jit_solution(5512264961647661236)
XLA Ops:
  0.6 77.6 %shard_map.122 = (bf16[64,4096]{1,0:T(8,128)(2,1)}, f32[1,1]{1,0:T(1,128)}) custom-call(bf16[64,4096]{1,0:T(8,128)(2,1)} %hidden.1, s32[1,32]{1,0:T(1,128)} %lens.1, s32[1,64]{1,0:T(1,128)} %bitcast.10, s32[7,64]{1,0:T(8,128)} %bitcast.9, f32[1,4096]{1,0:T(1,128)} %bitcast.7, bf16[4096,128]{1,0:T(8,128)(2,1)} %wq.1, bf16[4096,128]{1,0:T(8,128)(2,1)} %wkv.1, ...), custom_call_target="tpu_custom_call" | custom-call | tf_op jit(solution)/shard_map/pallas_call | solution.py:510
  78.2 1.9 %copy.15 = bf16[64,4096]{1,0:T(8,128)(2,1)} copy(bf16[64,4096]{1,0:T(8,128)(2,1)} %get-tuple-element.8) | data formatting | bytes 1048576

commit v3 on v2

--- a/solution.py
+++ b/solution.py
@@ -84,8 +84,8 @@
     N = own * T
     S = lens.shape[1]
     Q = positives.shape[1]
-    H = F // 2
-    HH = HD // 2
+    H = F // 4
+    HH = HD // 4
     root = math.sqrt(HD)
     t = lax.axis_index("tensor")
     g = lax.axis_index("dp")
@@ -93,20 +93,26 @@
     core = g % 2
     buddy = g + 1 - 2 * core
     mate = t + 1 - 2 * (t % 2)
+    z_mate = (zz + 1 - 2 * (zz % 2)) * 2 + core
+    quarter = (zz % 2) * 2 + core
+    far_quarter = (1 - zz % 2) * 2 + core
     even = t % 2 == 0
     peers = [lax.rem(t + k, T) for k in range(1, T)]
     sources = [lax.rem(t + T - k, T) for k in range(1, T)]
     slots = list(range(T))
     columns = pl.ds(pl.multiple_of(t * F, 128), F)
 
+    def block(p):
+        return pl.ds(pl.multiple_of(p * HD, 128), HD)
+
     own_copies = [
         pltpu.make_async_copy(hidden, hid_own, local_sem.at[0]),
         pltpu.make_async_copy(
             hidden.at[:, columns], hid_all.at[pl.ds(t * own, own)], local_sem.at[1]
         ),
-        pltpu.make_async_copy(wkv.at[pl.ds(t * F, F)], wkv_all.at[t], local_sem.at[2]),
-        pltpu.make_async_copy(wq.at[pl.ds(t * F, F)], wq_all.at[t], local_sem.at[3]),
-        pltpu.make_async_copy(wo.at[:, columns], wo_all.at[t], local_sem.at[4]),
+        pltpu.make_async_copy(wkv.at[pl.ds(t * F, F)], wkv_all.at[:, block(t)], local_sem.at[2]),
+        pltpu.make_async_copy(wq.at[pl.ds(t * F, F)], wq_all.at[:, block(t)], local_sem.at[3]),
+        pltpu.make_async_copy(wo.at[:, columns], wo_all.at[block(t)], local_sem.at[4]),
     ]
     for copy in own_copies:
         copy.start()
@@ -131,10 +137,10 @@
         waits.append(copy)
         return copy
 
-    def to_buddy(kind, k, src, dst):
+    def pass_on(kind, k, spot, target):
         copy = pltpu.make_async_remote_copy(
-            src_ref=src, dst_ref=dst, send_sem=fsend.at[kind, k], recv_sem=frecv.at[kind, k],
-            device_id=(buddy, t), device_id_type=MESH,
+            src_ref=spot, dst_ref=spot, send_sem=fsend.at[kind, k], recv_sem=frecv.at[kind, k],
+            device_id=(target, t), device_id_type=MESH,
         )
         copy.start()
         waits.append(copy)
@@ -150,17 +156,39 @@
     def cols(p):
         return pl.ds(pl.multiple_of(p * F, 128), F)
 
+    def tall_spot(ref):
+        def spot(source, part):
+            return ref.at[pl.ds(pl.multiple_of(part * H, H), H), block(source)]
+
+        return spot
+
+    def wide_spot(source, part):
+        return wo_all.at[pl.ds(pl.multiple_of(source * HD + part * HH, HH), HH)]
+
+    def own_tall(ref, p):
+        return ref.at[pl.ds(pl.multiple_of(p * F + quarter * H, H), H)]
+
+    def own_wide(p):
+        return wo.at[pl.ds(pl.multiple_of(quarter * HH, HH), HH), cols(p)]
+
+    def spread(kind, fetched, spot):
+        near, along = [], []
+        for k in rest:
+            fetched[k].wait_recv()
+            mine = spot(sources[k], quarter)
+            along.append(pass_on(kind, k, mine, z_mate))
+            near.append(pass_on(kind + 1, k, mine, buddy))
+        for k in rest:
+            along[k].wait_recv()
+            near.append(pass_on(kind + 2, k, spot(sources[k], far_quarter), buddy))
+        return near
+
+    wkv_spot, wq_spot = tall_spot(wkv_all), tall_spot(wq_all)
+    wkv_copies = [
+        to_peer(1, k, own_tall(wkv, peers[k]), wkv_spot(t, quarter)) for k in rest
+    ]
     hid_copies = [
         to_peer(0, k, hidden.at[:, cols(peers[k])], hid_all.at[my_rows]) for k in rest
-    ]
-
-    def half_rows(p):
-        return pl.ds(pl.multiple_of(p * F + core * H, H), H)
-
-    my_half = pl.ds(pl.multiple_of(core * H, H), H)
-    my_head_half = pl.ds(pl.multiple_of(core * HH, HH), HH)
-    wkv_copies = [
-        to_peer(1, k, wkv.at[half_rows(peers[k])], wkv_all.at[t, my_half]) for k in rest
     ]
 
     own_copies[0].wait()
@@ -192,14 +220,8 @@
     gain = in_gain[:, columns]
     ogain = out_gain[:, columns]
 
-    wkv_fwd = []
-    for k in rest:
-        wkv_copies[k].wait_recv()
-        spot = wkv_all.at[sources[k], my_half]
-        wkv_fwd.append(to_buddy(0, k, spot, spot))
-    wq_copies = [
-        to_peer(3, k, wq.at[half_rows(peers[k])], wq_all.at[t, my_half]) for k in rest
-    ]
+    wkv_near = spread(0, wkv_copies, wkv_spot)
+    wq_copies = [to_peer(3, k, own_tall(wq, peers[k]), wq_spot(t, quarter)) for k in rest]
 
     own_copies[1].wait()
     landed(hid_copies)
@@ -212,42 +234,33 @@
         inv_all[rows, :] = jnp.broadcast_to(inverse, (own, HD))
         normed[rows, :] = (hid_all[rows, :].astype(F32) * inverse * gain).astype(BF16)
     own_copies[2].wait()
-    landed(wkv_fwd)
-    for b in slots:
-        kvp_out[b] = nn(normed[...], wkv_all[b]).astype(BF16)
+    landed(wkv_near)
+    kvp_out[...] = nn(normed[...], wkv_all[...]).astype(BF16)
 
     def pair(p):
-        return pl.ds((p // 2) * 2, 2)
-
-    kvp_copies = [to_peer(4, k, kvp_out.at[pair(peers[k])], kvp_in.at[t]) for k in rest]
-    kvp_in[t] = kvp_out[pair(t)]
-
-    wq_fwd = []
-    for k in rest:
-        wq_copies[k].wait_recv()
-        spot = wq_all.at[sources[k], my_half]
-        wq_fwd.append(to_buddy(1, k, spot, spot))
-    wo_copies = [
-        to_peer(
-            5, k, wo.at[my_head_half, cols(peers[k])], wo_all.at[t, my_head_half]
-        )
-        for k in rest
+        return pl.ds(pl.multiple_of((p // 2) * (2 * HD), 256), 2 * HD)
+
+    kvp_copies = [
+        to_peer(4, k, kvp_out.at[:, pair(peers[k])], kvp_in.at[t]) for k in rest
     ]
+    kvp_in[t] = kvp_out[:, pair(t)]
+
+    wq_near = spread(3, wq_copies, wq_spot)
+    wo_copies = [to_peer(5, k, own_wide(peers[k]), wide_spot(t, quarter)) for k in rest]
     last16 = nn(last_hot, normed[...]).astype(BF16)
     hid_last = nn(last_hot, hid_all[...])
     own_copies[3].wait()
-    landed(wq_fwd)
-    for b in slots:
-        qp_out[b] = nn(last16, wq_all[b])
-    qp_copies = [to_peer(6, k, qp_out.at[peers[k]], qp_in.at[t]) for k in rest]
-    qp_in[t] = qp_out[t]
+    landed(wq_near)
+    qp_out[...] = nn(last16, wq_all[...])
+    qp_copies = [to_peer(6, k, qp_out.at[:, block(peers[k])], qp_in.at[t]) for k in rest]
+    qp_in[t] = qp_out[:, block(t)]
 
     landed(kvp_copies)
-    key_raw = kvp_in[0, 0].astype(F32)
-    value_raw = kvp_in[0, 1].astype(F32)
+    key_raw = kvp_in[0, :, 0:HD].astype(F32)
+    value_raw = kvp_in[0, :, HD : 2 * HD].astype(F32)
     for s in slots[1:]:
-        key_raw = key_raw + kvp_in[s, 0].astype(F32)
-        value_raw = value_raw + kvp_in[s, 1].astype(F32)
+        key_raw = key_raw + kvp_in[s, :, 0:HD].astype(F32)
+        value_raw = value_raw + kvp_in[s, :, HD : 2 * HD].astype(F32)
     value16 = value_raw.astype(BF16)
     key_unit, key_inverse, key_rot = head_forward(key_raw, kg, cos_key, sin_key)
     key16 = key_rot.astype(BF16)
@@ -262,21 +275,16 @@
     weight = jnp.where(inside, jnp.exp(scores - shift), 0.0)
     probs = weight / jnp.sum(weight, axis=-1, keepdims=True)
     probs16 = probs.astype(BF16)
-    attn_all[t] = nn(probs16, value16).astype(BF16)
-    attn_copies = [to_peer(7, k, attn_all.at[t], attn_all.at[t]) for k in rest]
-
-    wo_fwd = []
-    for k in rest:
-        wo_copies[k].wait_recv()
-        spot = wo_all.at[sources[k], my_head_half]
-        wo_fwd.append(to_buddy(2, k, spot, spot))
+    attn_all[:, block(t)] = nn(probs16, value16).astype(BF16)
+    my_attn = attn_all.at[:, block(t)]
+    attn_copies = [to_peer(7, k, my_attn, my_attn) for k in rest]
+
+    wo_near = spread(6, wo_copies, wide_spot)
     own_copies[4].wait()
-    landed(wo_fwd)
+    landed(wo_near)
     landed(attn_copies)
 
-    resid = hid_last
-    for s in slots:
-        resid = resid + nn(attn_all[s], wo_all[s])
+    resid = hid_last + nn(attn_all[...], wo_all[...])
     my_seqs = pl.ds(pl.multiple_of(g * S, S), S)
     embeds[my_seqs, :] = (resid * ogain).astype(BF16)
     z_copies = []
@@ -378,10 +386,9 @@
     d_resid16 = d_resid.astype(BF16)
     d_resid_low = (d_resid - d_resid16.astype(F32)).astype(BF16)
 
-    for b in slots:
-        dap_out[b] = nt(d_resid16, wo_all[b])
-    dap_copies = [to_peer(10, k, dap_out.at[peers[k]], dap_in.at[t]) for k in rest]
-    dap_in[t] = dap_out[t]
+    dap_out[...] = nt(d_resid16, wo_all[...])
+    dap_copies = [to_peer(10, k, dap_out.at[:, block(peers[k])], dap_in.at[t]) for k in rest]
+    dap_in[t] = dap_out[:, block(t)]
     eye_n = iota((N, N), 0) == iota((N, N), 1)
     eye16 = onehot(eye_n)
     probs16_t = nt(eye16, probs16).astype(BF16)
@@ -407,8 +414,9 @@
     d_query16 = head_backward(
         d_query_rot, query_unit, query_inverse, qg, cos_query, sin_query
     ).astype(BF16)
-    dq_all[t] = d_query16
-    dq_copies = [to_peer(11, k, dq_all.at[t], dq_all.at[t]) for k in rest]
+    dq_all[:, block(t)] = d_query16
+    my_dq = dq_all.at[:, block(t)]
+    dq_copies = [to_peer(11, k, my_dq, my_dq) for k in rest]
     query_rows = nn(
         last_hot_t.astype(F32), d_query16.astype(F32) * query_raw, EXACT
     )
@@ -416,45 +424,44 @@
     whole = jnp.where(even, d_key_rot, d_value) + pair_in[...].astype(F32)
     d_key_raw = head_backward(whole, key_unit, key_inverse, kg, cos_key, sin_key)
     column16 = jnp.where(even, d_key_raw, whole).astype(BF16)
-    dkv_all[t] = column16
-    dkv_copies = [to_peer(12, k, dkv_all.at[t], dkv_all.at[t]) for k in rest]
+    dkv_all[:, block(t)] = column16
+    my_dkv = dkv_all.at[:, block(t)]
+    dkv_copies = [to_peer(12, k, my_dkv, my_dkv) for k in rest]
     raw = jnp.where(even, key_raw, value_raw)
     rows_all[t] = nt(
         jnp.ones((8, HD), F32), column16.astype(F32) * raw + query_rows, EXACT
     )
-    row_copies = [to_peer(13, k, rows_all.at[t], rows_all.at[t]) for k in rest]
+    row_copies = [to_peer(8, k, rows_all.at[t], rows_all.at[t]) for k in rest]
     landed(dq_copies)
-    landed(dkv_copies)
+    dq_rows = nn(last_hot_t, dq_all[...]).astype(BF16)
     landed(row_copies)
-
     row_sums = rows_all[0]
     for s in slots[1:]:
         row_sums = row_sums + rows_all[s]
-    out_copies = []
-    for k, p in list(enumerate(peers)) + [(None, t)]:
-        rows = pl.ds(pl.multiple_of(p * own, own), own)
-        hit = iota((own, N), 1) == p * own + iota((own, N), 0)
-        mean = jnp.sum(jnp.where(hit, row_sums[0:1, :], 0.0), axis=1, keepdims=True) / D
-        last_here = onehot(
-            (iota((own, S), 0) + p * own).astype(F32) == ends_row - 1.0
+    mean = jnp.sum(jnp.where(eye_n, row_sums[0:1, :], 0.0), axis=1, keepdims=True) / D
+    inverse = inv_all[:, 0:1]
+    landed(dkv_copies)
+    out_copies, local = [], []
+    FC = F // 2
+    for c in range(2):
+        span = slice(c * FC, (c + 1) * FC)
+        there = pl.ds(pl.multiple_of(t * F + c * FC, 128), FC)
+        d_normed = nt(dkv_all[...], wkv_all[span, :]) + nt(dq_rows, wq_all[span, :])
+        unit = hid_all[:, span].astype(F32) * inverse
+        grad = inverse * (d_normed * gain[:, span] - unit * mean)
+        grad = grad + nn(last_hot_t, d_resid16[:, span]) + nn(last_hot_t, d_resid_low[:, span])
+        out16[:, span] = grad.astype(BF16)
+        for k in rest:
+            rows = pl.ds(pl.multiple_of(peers[k] * own, own), own)
+            out_copies.append(to_peer(13 + c, k, out16.at[rows, span], out.at[:, there]))
+        copy = pltpu.make_async_copy(
+            out16.at[my_rows, span], out.at[:, there], local_sem.at[5 + c]
         )
-        d_normed = nt(dkv_all[0, rows], wkv_all[0])
-        for b in slots:
-            if b > 0:
-                d_normed = d_normed + nt(dkv_all[b, rows], wkv_all[b])
-            d_normed = d_normed + nt(nn(last_here, dq_all[b]).astype(BF16), wq_all[b])
-        inverse = inv_all[rows, 0:1]
-        unit = hid_all[rows, :].astype(F32) * inverse
-        grad = inverse * (d_normed * gain - unit * mean)
-        grad = grad + nn(last_here, d_resid16) + nn(last_here, d_resid_low)
-        out16[rows, :] = grad.astype(BF16)
-        if k is None:
-            local = pltpu.make_async_copy(out16.at[rows], out.at[:, columns], local_sem.at[5])
-            local.start()
-        else:
-            out_copies.append(to_peer(14, k, out16.at[rows], out.at[:, columns]))
+        copy.start()
+        local.append(copy)
     landed(out_copies)
-    local.wait()
+    for copy in local:
+        copy.wait()
     for copy in waits:
         copy.wait_send()
 
@@ -479,29 +486,29 @@
         pltpu.VMEM((T, 8, HD), F32),
         pltpu.VMEM((N, HD), F32),
         pltpu.VMEM((N, F), BF16),
-        pltpu.VMEM((T, F, HD), BF16),
-        pltpu.VMEM((T, F, HD), BF16),
-        pltpu.VMEM((T, HD, F), BF16),
-        pltpu.VMEM((T, N, HD), BF16),
-        pltpu.VMEM((T, 2, N, HD), BF16),
+        pltpu.VMEM((F, T * HD), BF16),
+        pltpu.VMEM((F, T * HD), BF16),
+        pltpu.VMEM((T * HD, F), BF16),
+        pltpu.VMEM((N, T * HD), BF16),
+        pltpu.VMEM((T, N, 2 * HD), BF16),
+        pltpu.VMEM((S, T * HD), F32),
         pltpu.VMEM((T, S, HD), F32),
-        pltpu.VMEM((T, S, HD), F32),
-        pltpu.VMEM((T, S, HD), BF16),
+        pltpu.VMEM((S, T * HD), BF16),
         pltpu.VMEM((G * S, F), BF16),
         pltpu.VMEM((T, Q + 8, G * S), F32),
-        pltpu.VMEM((T, S, HD), F32),
+        pltpu.VMEM((S, T * HD), F32),
         pltpu.VMEM((T, S, HD), F32),
         pltpu.VMEM((N, HD), BF16),
         pltpu.VMEM((N, HD), BF16),
-        pltpu.VMEM((T, N, HD), BF16),
-        pltpu.VMEM((T, S, HD), BF16),
+        pltpu.VMEM((N, T * HD), BF16),
+        pltpu.VMEM((S, T * HD), BF16),
         pltpu.VMEM((T, 8, N), F32),
         pltpu.VMEM((N, F), BF16),
-        pltpu.SemaphoreType.DMA((6,)),
+        pltpu.SemaphoreType.DMA((7,)),
         pltpu.SemaphoreType.DMA((15, T - 1)),
         pltpu.SemaphoreType.DMA((15, T - 1)),
-        pltpu.SemaphoreType.DMA((3, T - 1)),
-        pltpu.SemaphoreType.DMA((3, T - 1)),
+        pltpu.SemaphoreType.DMA((9, T - 1)),
+        pltpu.SemaphoreType.DMA((9, T - 1)),
         pltpu.SemaphoreType.DMA((Z - 1,)),
         pltpu.SemaphoreType.DMA((Z - 1,)),
         pltpu.SemaphoreType.DMA((Z + 1,)),

time: 82.1 us -> 78.1 us (0.951)
  Pallas kernels: 77.6 us -> 73.6 us
    pallas_call x1, Pallas kernels: 77.6 us -> 73.6 us  [on_device(): pl.pallas_call(functools.partial(kernel, T, G), out_shape=(jax.ShapeDtype...]
where the time goes in v3:
time: 78.1 us; the launch traced here: 77.8 us
  Pallas kernels  73.6 us (94%)
  between operations  2.34 us (3%)
  local copies, waits for them, and re-layouts  1.87 us (2%)
    pallas_call x1, Pallas kernels, on_device(): pl.pallas_call(functools.partial(kernel, T, G), out_shape=(jax.ShapeDtype...  73.6 us
    unnamed x1, local copies, waits for them, and re-layouts  1.87 us

profile of v3, /device:TPU:0, one launch (start us, length us, event | category | flops | bytes accessed | tf_op | source)
XLA Modules:
  0.0 77.8 jit_solution(15972945473180445843)
XLA Ops:
  0.6 73.6 %shard_map.122 = (bf16[64,4096]{1,0:T(8,128)(2,1)}, f32[1,1]{1,0:T(1,128)}) custom-call(bf16[64,4096]{1,0:T(8,128)(2,1)} %hidden.1, s32[1,32]{1,0:T(1,128)} %lens.1, s32[1,64]{1,0:T(1,128)} %bitcast.10, s32[7,64]{1,0:T(8,128)} %bitcast.9, f32[1,4096]{1,0:T(1,128)} %bitcast.7, bf16[4096,128]{1,0:T(8,128)(2,1)} %wq.1, bf16[4096,128]{1,0:T(8,128)(2,1)} %wkv.1, ...), custom_call_target="tpu_custom_call" | custom-call | tf_op jit(solution)/shard_map/pallas_call | solution.py:517
  74.3 1.9 %copy.15 = bf16[64,4096]{1,0:T(8,128)(2,1)} copy(bf16[64,4096]{1,0:T(8,128)(2,1)} %get-tuple-element.8) | data formatting | bytes 1048576

commit v4 on v3

--- a/solution.py
+++ b/solution.py
@@ -12,6 +12,7 @@
 EPSILON = 1e-06
 SOFTMAX_TEMPER = 0.05
 LOSS_MULTIPLIER = 8192.0
+CHUNKS = 4
 ROPE_BASE = 1000000.0
 
 F32 = jnp.float32
@@ -69,11 +70,11 @@
 
 def kernel(
     tensors, groups,
-    hidden, lens, positives, negatives, in_gain, wq, wkv, q_gain, k_gain, wo, out_gain,
-    out, loss,
+    hidden, lens_in, positives_in, negatives_in, in_gain, wq, wkv, q_gain, k_gain, wo, out_gain,
+    out, loss, lens, positives, negatives, gains, head_gains,
     hid_own, hid_all, inv_rows, inv_all, normed, wkv_all, wq_all, wo_all,
-    kvp_out, kvp_in, qp_out, qp_in, attn_all, embeds, logit_all,
-    dap_out, dap_in, pair_out, pair_in, dkv_all, dq_all, rows_all, out16,
+    kvp_out, kvp_in, qp_out, qp_in, attn_all, embeds, logit_all, stats_all,
+    dap_out, dap_in, dkv_all, dq_all, rows_all, addend, out16,
     local_sem, tsend, trecv, fsend, frecv, zsend, zrecv, psend, precv,
 ):
     T, G = tensors, groups
@@ -82,8 +83,8 @@
     F = D // T
     HD = wq.shape[1]
     N = own * T
-    S = lens.shape[1]
-    Q = positives.shape[1]
+    S = lens_in.shape[1]
+    Q = positives_in.shape[1]
     H = F // 4
     HH = HD // 4
     root = math.sqrt(HD)
@@ -92,7 +93,6 @@
     zz = g // 2
     core = g % 2
     buddy = g + 1 - 2 * core
-    mate = t + 1 - 2 * (t % 2)
     z_mate = (zz + 1 - 2 * (zz % 2)) * 2 + core
     quarter = (zz % 2) * 2 + core
     far_quarter = (1 - zz % 2) * 2 + core
@@ -113,6 +113,13 @@
         pltpu.make_async_copy(wkv.at[pl.ds(t * F, F)], wkv_all.at[:, block(t)], local_sem.at[2]),
         pltpu.make_async_copy(wq.at[pl.ds(t * F, F)], wq_all.at[:, block(t)], local_sem.at[3]),
         pltpu.make_async_copy(wo.at[:, columns], wo_all.at[block(t)], local_sem.at[4]),
+        pltpu.make_async_copy(lens_in, lens, local_sem.at[5]),
+        pltpu.make_async_copy(positives_in, positives, local_sem.at[6]),
+        pltpu.make_async_copy(negatives_in, negatives, local_sem.at[7]),
+        pltpu.make_async_copy(in_gain.at[:, columns], gains.at[0], local_sem.at[8]),
+        pltpu.make_async_copy(out_gain.at[:, columns], gains.at[1], local_sem.at[9]),
+        pltpu.make_async_copy(q_gain, head_gains.at[0], local_sem.at[10]),
+        pltpu.make_async_copy(k_gain, head_gains.at[1], local_sem.at[11]),
     ]
     for copy in own_copies:
         copy.start()
@@ -199,6 +206,9 @@
     )
     inv_copies = [to_peer(2, k, inv_rows.at[t], inv_rows.at[t]) for k in rest]
 
+    for copy in own_copies[5:]:
+        copy.wait()
+
     lens_row = lens[...].astype(F32)
     square_r, square_c = iota((S, S), 0), iota((S, S), 1)
     lens_col = jnp.sum(jnp.where(square_r == square_c, lens_row, 0.0), axis=1, keepdims=True)
@@ -207,18 +217,23 @@
     starts_col, starts_row = ends_col - lens_col, ends_row - lens_row
     token_row = iota((S, N), 1).astype(F32)
     token_col = iota((N, S), 0).astype(F32)
-    inside = (token_row >= starts_col) & (token_row < ends_col)
+    both_starts = jnp.concatenate([starts_col, starts_col], axis=0)
+    both_ends = jnp.concatenate([ends_col, ends_col], axis=0)
+    both_row = iota((2 * S, N), 1).astype(F32)
+    inside = (both_row >= both_starts) & (both_row < both_ends)
     inside_t = (token_col >= starts_row) & (token_col < ends_row)
     offset = jnp.sum(jnp.where(inside_t, starts_row, 0.0), axis=1, keepdims=True)
     position = iota((N, 1), 0).astype(F32) - offset
-    last_hot = onehot(token_row == ends_col - 1.0)
+    is_last = token_row == ends_col - 1.0
+    last_hot = onehot(is_last)
     last_hot_t = onehot(token_col == ends_row - 1.0)
     cos_key, sin_key = rope_tables(position, HD)
-    cos_query, sin_query = rope_tables(lens_col - 1.0, HD)
-    qg, kg = q_gain[...], k_gain[...]
+    cos_query, sin_query = rope_tables(both_ends - both_starts - 1.0, HD)
+    qg, kg = head_gains[0], head_gains[1]
     shift = root * jnp.max(qg, axis=1, keepdims=True) * jnp.max(kg, axis=1, keepdims=True)
-    gain = in_gain[:, columns]
-    ogain = out_gain[:, columns]
+    gain, ogain = gains[0], gains[1]
+    eye_n = iota((N, N), 0) == iota((N, N), 1)
+    eye16 = onehot(eye_n)
 
     wkv_near = spread(0, wkv_copies, wkv_spot)
     wq_copies = [to_peer(3, k, own_tall(wq, peers[k]), wq_spot(t, quarter)) for k in rest]
@@ -246,14 +261,15 @@
     kvp_in[t] = kvp_out[:, pair(t)]
 
     wq_near = spread(3, wq_copies, wq_spot)
-    wo_copies = [to_peer(5, k, own_wide(peers[k]), wide_spot(t, quarter)) for k in rest]
     last16 = nn(last_hot, normed[...]).astype(BF16)
-    hid_last = nn(last_hot, hid_all[...])
     own_copies[3].wait()
     landed(wq_near)
     qp_out[...] = nn(last16, wq_all[...])
-    qp_copies = [to_peer(6, k, qp_out.at[:, block(peers[k])], qp_in.at[t]) for k in rest]
-    qp_in[t] = qp_out[:, block(t)]
+    qp_copies = [to_peer(6, k, qp_out.at[:, pair(peers[k])], qp_in.at[t]) for k in rest]
+    qp_in[t] = qp_out[:, pair(t)]
+    wo_copies = [to_peer(5, k, own_wide(peers[k]), wide_spot(t, quarter)) for k in rest]
+    hid_last = nn(last_hot, hid_all[...])
+    inverse_last = nn(last_hot.astype(F32), inv_all[...], EXACT)[:, 0:1]
 
     landed(kvp_copies)
     key_raw = kvp_in[0, :, 0:HD].astype(F32)
@@ -269,15 +285,17 @@
     query_raw = qp_in[0]
     for s in slots[1:]:
         query_raw = query_raw + qp_in[s]
+    query_raw = jnp.concatenate([query_raw[:, :HD], query_raw[:, HD:]], axis=0)
     query_unit, query_inverse, query_rot = head_forward(query_raw, qg, cos_query, sin_query)
     query16 = query_rot.astype(BF16)
     scores = nt(query16, key16) / root
     weight = jnp.where(inside, jnp.exp(scores - shift), 0.0)
     probs = weight / jnp.sum(weight, axis=-1, keepdims=True)
     probs16 = probs.astype(BF16)
-    attn_all[:, block(t)] = nn(probs16, value16).astype(BF16)
+    attn = nn(probs16, value16)
+    attn_all[:, block(t)] = jnp.where(even, attn[:S], attn[S:]).astype(BF16)
     my_attn = attn_all.at[:, block(t)]
-    attn_copies = [to_peer(7, k, my_attn, my_attn) for k in rest]
+    attn_copies = [to_peer(10, k, my_attn, my_attn) for k in rest]
 
     wo_near = spread(6, wo_copies, wide_spot)
     own_copies[4].wait()
@@ -332,6 +350,8 @@
     row_s = iota((S, Q), 0)
     own_q = (row_s < QDEV) & (iota((S, Q), 1) == g * QDEV + row_s)
     own_p = iota((S, E), 1) == g * S + iota((S, E), 0)
+    own_q16, own_p16 = onehot(own_q), onehot(own_p)
+    plain_gain = 1.0 / ogain
 
     for k in range(1, Z):
         z_copies[k - 1].wait_recv()
@@ -340,21 +360,23 @@
     landed(shared)
 
     queries = nn(pick_q, embeds[...]).astype(BF16)
-    plain = (embeds[...].astype(F32) * (1.0 / ogain)).astype(BF16)
+    logit_all[t] = nt(queries, embeds[...])
+    logit_copies = [to_peer(9, k, logit_all.at[t], logit_all.at[t]) for k in rest]
+    plain = (embeds[...].astype(F32) * plain_gain).astype(BF16)
     plain_sq = jnp.sum(jnp.where(eye_e, nt(plain, plain), 0.0), axis=0, keepdims=True)
     scaled_sq = jnp.sum(
         jnp.where(eye_e, nt(embeds[...], embeds[...]), 0.0), axis=0, keepdims=True
     )
-    logit_all[t, 0:Q] = nt(queries, embeds[...])
-    logit_all[t, Q : Q + 8] = jnp.where(iota((8, E), 0) == 0, plain_sq, scaled_sq)
-    logit_copies = [to_peer(9, k, logit_all.at[t], logit_all.at[t]) for k in rest]
+    stats_all[t] = jnp.where(iota((8, E), 0) == 0, plain_sq, scaled_sq)
+    stats_copies = [to_peer(7, k, stats_all.at[t], stats_all.at[t]) for k in rest]
     landed(logit_copies)
-    summed = logit_all[0]
+    landed(stats_copies)
+    raw_dots, stats = logit_all[0], stats_all[0]
     for s in slots[1:]:
-        summed = summed + logit_all[s]
-    raw_dots = summed[0:Q]
-    inverse_row = lax.rsqrt(summed[Q : Q + 1] / D + EPSILON)
-    final_row = lax.rsqrt(inverse_row * inverse_row * summed[Q + 1 : Q + 2] + EPSILON)
+        raw_dots = raw_dots + logit_all[s]
+        stats = stats + stats_all[s]
+    inverse_row = lax.rsqrt(stats[0:1] / D + EPSILON)
+    final_row = lax.rsqrt(inverse_row * inverse_row * stats[1:2] + EPSILON)
     scale_row = inverse_row * final_row
     scale_q = jnp.sum(jnp.where(pick, scale_row, 0.0), axis=1, keepdims=True)
     resid_inverse = jnp.sum(jnp.where(own_p, inverse_row, 0.0), axis=1, keepdims=True)
@@ -365,75 +387,69 @@
     logits = dots_q * scale_row / SOFTMAX_TEMPER
     grown = jnp.where(allowed, jnp.exp(logits - 1.0 / SOFTMAX_TEMPER), 0.0)
     totals = jnp.sum(grown, axis=1, keepdims=True)
-    target = jnp.sum(jnp.where(pos_hot, logits, 0.0), axis=1, keepdims=True)
-    each = jnp.log(totals) + 1.0 / SOFTMAX_TEMPER - target
-    loss[0, 0] = jnp.sum(each) / Q
     factor = LOSS_MULTIPLIER / (Q * SOFTMAX_TEMPER)
     coef = factor * (grown / totals - positive_f)
     coef_q16 = (coef * scale_row).astype(BF16)
     coef_p16 = (coef * scale_q).astype(BF16)
-    coef_q = nn(onehot(own_q), coef_q16).astype(BF16)
-    coef_p = nt(onehot(own_p), coef_p16).astype(BF16)
+    coef_q = nn(own_q16, coef_q16).astype(BF16)
+    coef_p = nt(own_p16, coef_p16).astype(BF16)
     d_embed = nn(coef_q, embeds[...]) + nn(coef_p, queries)
-    along_q = coef_q16.astype(F32) * dots_q
-    along_p = coef_p16.astype(F32) * dots_p
-    inner = jnp.sum(nn(onehot(own_q, F32), along_q, EXACT), axis=1, keepdims=True) + jnp.sum(
-        nt(onehot(own_p, F32), along_p, EXACT), axis=1, keepdims=True
+    along_q = jnp.sum(coef_q16.astype(F32) * dots_q, axis=1, keepdims=True)
+    along_p = jnp.sum(coef_p16.astype(F32) * dots_p, axis=0, keepdims=True)
+    along_q = jnp.sum(jnp.where(eye_q, along_q, 0.0), axis=0, keepdims=True)
+    inner = jnp.sum(jnp.where(own_q, along_q, 0.0), axis=1, keepdims=True) + jnp.sum(
+        jnp.where(own_p, along_p, 0.0), axis=1, keepdims=True
     )
     d_final = final_inverse * (d_embed - embed * inner)
     middle = inner * (EPSILON / D) * final_inverse * final_inverse
     d_resid = resid_inverse * (ogain * d_final - resid_unit * middle)
     d_resid16 = d_resid.astype(BF16)
-    d_resid_low = (d_resid - d_resid16.astype(F32)).astype(BF16)
 
     dap_out[...] = nt(d_resid16, wo_all[...])
-    dap_copies = [to_peer(10, k, dap_out.at[:, block(peers[k])], dap_in.at[t]) for k in rest]
-    dap_in[t] = dap_out[:, block(t)]
-    eye_n = iota((N, N), 0) == iota((N, N), 1)
-    eye16 = onehot(eye_n)
+    dap_copies = [to_peer(11, k, dap_out.at[:, pair(peers[k])], dap_in.at[t]) for k in rest]
+    dap_in[t] = dap_out[:, pair(t)]
+    target = jnp.sum(jnp.where(pos_hot, logits, 0.0), axis=1, keepdims=True)
+    loss[0, 0] = jnp.sum(jnp.log(totals) + 1.0 / SOFTMAX_TEMPER - target) / Q
     probs16_t = nt(eye16, probs16).astype(BF16)
     landed(dap_copies)
     d_attn = dap_in[0]
     for s in slots[1:]:
         d_attn = d_attn + dap_in[s]
-    d_attn16 = d_attn.astype(BF16)
+    d_attn16 = jnp.concatenate([d_attn[:, :HD], d_attn[:, HD:]], axis=0).astype(BF16)
     d_probs = nt(d_attn16, value16)
     d_scores16 = (
         probs * (d_probs - jnp.sum(probs * d_probs, axis=-1, keepdims=True)) / root
     ).astype(BF16)
     d_key_rot = nn(nt(eye16, d_scores16).astype(BF16), query16)
     d_value = nn(probs16_t, d_attn16)
-    pair_out[...] = jnp.where(even, d_value, d_key_rot).astype(BF16)
-    pair_copy = pltpu.make_async_remote_copy(
-        src_ref=pair_out, dst_ref=pair_in, send_sem=psend.at[Z], recv_sem=precv.at[Z],
-        device_id=(g, mate), device_id_type=MESH,
-    )
-    pair_copy.start()
-    waits.append(pair_copy)
-    d_query_rot = nn(d_scores16, key16)
-    d_query16 = head_backward(
-        d_query_rot, query_unit, query_inverse, qg, cos_query, sin_query
-    ).astype(BF16)
-    dq_all[:, block(t)] = d_query16
-    my_dq = dq_all.at[:, block(t)]
-    dq_copies = [to_peer(11, k, my_dq, my_dq) for k in rest]
-    query_rows = nn(
-        last_hot_t.astype(F32), d_query16.astype(F32) * query_raw, EXACT
-    )
-    pair_copy.wait_recv()
-    whole = jnp.where(even, d_key_rot, d_value) + pair_in[...].astype(F32)
-    d_key_raw = head_backward(whole, key_unit, key_inverse, kg, cos_key, sin_key)
-    column16 = jnp.where(even, d_key_raw, whole).astype(BF16)
+    d_key_raw = head_backward(d_key_rot, key_unit, key_inverse, kg, cos_key, sin_key)
+    column16 = jnp.where(even, d_key_raw, d_value).astype(BF16)
     dkv_all[:, block(t)] = column16
     my_dkv = dkv_all.at[:, block(t)]
     dkv_copies = [to_peer(12, k, my_dkv, my_dkv) for k in rest]
+    d_query_rot = nn(d_scores16, key16)
+    d_query_raw = head_backward(
+        d_query_rot, query_unit, query_inverse, qg, cos_query, sin_query
+    )
+    d_query16 = jnp.where(even, d_query_raw[:S], d_query_raw[S:]).astype(BF16)
+    dq_all[:, block(t)] = d_query16
+    my_dq = dq_all.at[:, block(t)]
+    dq_copies = [to_peer(13, k, my_dq, my_dq) for k in rest]
     raw = jnp.where(even, key_raw, value_raw)
-    rows_all[t] = nt(
-        jnp.ones((8, HD), F32), column16.astype(F32) * raw + query_rows, EXACT
+    kv_sums = jnp.sum(column16.astype(F32) * raw, axis=1, keepdims=True)
+    own_query = jnp.where(even, query_raw[:S], query_raw[S:])
+    query_sums = jnp.sum(d_query16.astype(F32) * own_query, axis=1, keepdims=True)
+    rows_all[t] = jnp.broadcast_to(
+        jnp.sum(jnp.where(eye_n, kv_sums, 0.0), axis=0, keepdims=True)
+        + jnp.sum(jnp.where(is_last, query_sums, 0.0), axis=0, keepdims=True),
+        (8, N),
     )
     row_copies = [to_peer(8, k, rows_all.at[t], rows_all.at[t]) for k in rest]
     landed(dq_copies)
-    dq_rows = nn(last_hot_t, dq_all[...]).astype(BF16)
+    extra = inverse_last * gain * nt(dq_all[...], wq_all[...]) + d_resid
+    extra16 = extra.astype(BF16)
+    extra_low = (extra - extra16.astype(F32)).astype(BF16)
+    addend[...] = nn(last_hot_t, extra16) + nn(last_hot_t, extra_low)
     landed(row_copies)
     row_sums = rows_all[0]
     for s in slots[1:]:
@@ -442,20 +458,19 @@
     inverse = inv_all[:, 0:1]
     landed(dkv_copies)
     out_copies, local = [], []
-    FC = F // 2
-    for c in range(2):
+    FC = F // CHUNKS if F % (128 * CHUNKS) == 0 else F // 2
+    for c in range(F // FC):
         span = slice(c * FC, (c + 1) * FC)
         there = pl.ds(pl.multiple_of(t * F + c * FC, 128), FC)
-        d_normed = nt(dkv_all[...], wkv_all[span, :]) + nt(dq_rows, wq_all[span, :])
+        d_normed = nt(dkv_all[...], wkv_all[span, :])
         unit = hid_all[:, span].astype(F32) * inverse
-        grad = inverse * (d_normed * gain[:, span] - unit * mean)
-        grad = grad + nn(last_hot_t, d_resid16[:, span]) + nn(last_hot_t, d_resid_low[:, span])
+        grad = inverse * (d_normed * gain[:, span] - unit * mean) + addend[:, span]
         out16[:, span] = grad.astype(BF16)
         for k in rest:
             rows = pl.ds(pl.multiple_of(peers[k] * own, own), own)
-            out_copies.append(to_peer(13 + c, k, out16.at[rows, span], out.at[:, there]))
+            out_copies.append(to_peer(14 + c, k, out16.at[rows, span], out.at[:, there]))
         copy = pltpu.make_async_copy(
-            out16.at[my_rows, span], out.at[:, there], local_sem.at[5 + c]
+            out16.at[my_rows, span], out.at[:, there], local_sem.at[12 + c]
         )
         copy.start()
         local.append(copy)
@@ -478,9 +493,14 @@
     S = lengths.shape[1]
     Q = positives.shape[0]
     Z = G // 2
-    vmem = pl.BlockSpec(memory_space=pltpu.VMEM)
+    hbm = pl.BlockSpec(memory_space=pltpu.HBM)
     anywhere = pl.BlockSpec(memory_space=pl.ANY)
     scratch = [
+        pltpu.VMEM((1, S), jnp.int32),
+        pltpu.VMEM((1, Q), jnp.int32),
+        pltpu.VMEM((negatives.shape[1], Q), jnp.int32),
+        pltpu.VMEM((2, 1, F), F32),
+        pltpu.VMEM((2, 1, HD), F32),
         pltpu.VMEM((own, D), BF16),
         pltpu.VMEM((N, F), BF16),
         pltpu.VMEM((T, 8, HD), F32),
@@ -492,27 +512,27 @@
         pltpu.VMEM((N, T * HD), BF16),
         pltpu.VMEM((T, N, 2 * HD), BF16),
         pltpu.VMEM((S, T * HD), F32),
-        pltpu.VMEM((T, S, HD), F32),
+        pltpu.VMEM((T, S, 2 * HD), F32),
         pltpu.VMEM((S, T * HD), BF16),
         pltpu.VMEM((G * S, F), BF16),
-        pltpu.VMEM((T, Q + 8, G * S), F32),
+        pltpu.VMEM((T, Q, G * S), F32),
+        pltpu.VMEM((T, 8, G * S), F32),
         pltpu.VMEM((S, T * HD), F32),
-        pltpu.VMEM((T, S, HD), F32),
-        pltpu.VMEM((N, HD), BF16),
-        pltpu.VMEM((N, HD), BF16),
+        pltpu.VMEM((T, S, 2 * HD), F32),
         pltpu.VMEM((N, T * HD), BF16),
         pltpu.VMEM((S, T * HD), BF16),
         pltpu.VMEM((T, 8, N), F32),
+        pltpu.VMEM((N, F), F32),
         pltpu.VMEM((N, F), BF16),
-        pltpu.SemaphoreType.DMA((7,)),
-        pltpu.SemaphoreType.DMA((15, T - 1)),
-        pltpu.SemaphoreType.DMA((15, T - 1)),
+        pltpu.SemaphoreType.DMA((12 + CHUNKS,)),
+        pltpu.SemaphoreType.DMA((14 + CHUNKS, T - 1)),
+        pltpu.SemaphoreType.DMA((14 + CHUNKS, T - 1)),
         pltpu.SemaphoreType.DMA((9, T - 1)),
         pltpu.SemaphoreType.DMA((9, T - 1)),
-        pltpu.SemaphoreType.DMA((Z - 1,)),
-        pltpu.SemaphoreType.DMA((Z - 1,)),
-        pltpu.SemaphoreType.DMA((Z + 1,)),
-        pltpu.SemaphoreType.DMA((Z + 1,)),
+        pltpu.SemaphoreType.DMA((Z,)),
+        pltpu.SemaphoreType.DMA((Z,)),
+        pltpu.SemaphoreType.DMA((Z,)),
+        pltpu.SemaphoreType.DMA((Z,)),
     ]
     d_hidden, loss = pl.pallas_call(
         functools.partial(kernel, T, G),
@@ -520,9 +540,7 @@
             jax.ShapeDtypeStruct((own, D), BF16),
             jax.ShapeDtypeStruct((1, 1), F32),
         ),
-        in_specs=[
-            anywhere, vmem, vmem, vmem, vmem, anywhere, anywhere, vmem, vmem, anywhere, vmem
-        ],
+        in_specs=[hbm] * 11,
         out_specs=(anywhere, pl.BlockSpec(memory_space=pltpu.SMEM)),
         scratch_shapes=scratch,
         compiler_params=pltpu.CompilerParams(

time: 78.1 us -> 77 us (0.986)
  Pallas kernels: 73.6 us -> 72.2 us
    pallas_call x1, Pallas kernels: 73.6 us -> 72.2 us  [on_device(): pl.pallas_call(functools.partial(kernel, T, G), out_shape=(jax.ShapeDtype...]
where the time goes in v4:
time: 77 us; the launch traced here: 76.4 us
  Pallas kernels  72.2 us (94%)
  between operations  2.34 us (3%)
  local copies, waits for them, and re-layouts  1.87 us (2%)
    pallas_call x1, Pallas kernels, on_device(): pl.pallas_call(functools.partial(kernel, T, G), out_shape=(jax.ShapeDtype...  72.2 us
    unnamed x1, local copies, waits for them, and re-layouts  1.87 us

profile of v4, /device:TPU:0, one launch (start us, length us, event | category | flops | bytes accessed | tf_op | source)
XLA Modules:
  0.0 76.4 jit_solution(13365995464159959458)
XLA Ops:
  0.6 72.2 %shard_map.122 = (bf16[64,4096]{1,0:T(8,128)(2,1)}, f32[1,1]{1,0:T(1,128)}) custom-call(bf16[64,4096]{1,0:T(8,128)(2,1)} %hidden.1, s32[1,32]{1,0:T(1,128)} %lens_in.1, s32[1,64]{1,0:T(1,128)} %bitcast.10, s32[7,64]{1,0:T(8,128)} %bitcast.9, f32[1,4096]{1,0:T(1,128)} %bitcast.7, bf16[4096,128]{1,0:T(8,128)(2,1)} %wq.1, bf16[4096,128]{1,0:T(8,128)(2,1)} %wkv.1, ...), custom_call_target="tpu_custom_call" | custom-call | tf_op jit(solution)/shard_map/pallas_call | solution.py:537
  72.9 1.9 %copy.15 = bf16[64,4096]{1,0:T(8,128)(2,1)} copy(bf16[64,4096]{1,0:T(8,128)(2,1)} %get-tuple-element.8) | data formatting | bytes 1048576

commit v5 on v4

--- a/solution.py
+++ b/solution.py
@@ -185,10 +185,14 @@
             mine = spot(sources[k], quarter)
             along.append(pass_on(kind, k, mine, z_mate))
             near.append(pass_on(kind + 1, k, mine, buddy))
+        return near, along
+
+    def finish(kind, begun, spot):
+        near, along = begun
         for k in rest:
             along[k].wait_recv()
             near.append(pass_on(kind + 2, k, spot(sources[k], far_quarter), buddy))
-        return near
+        landed(near)
 
     wkv_spot, wq_spot = tall_spot(wkv_all), tall_spot(wq_all)
     wkv_copies = [
@@ -206,6 +210,7 @@
     )
     inv_copies = [to_peer(2, k, inv_rows.at[t], inv_rows.at[t]) for k in rest]
 
+    wkv_begun = spread(0, wkv_copies, wkv_spot)
     for copy in own_copies[5:]:
         copy.wait()
 
@@ -235,9 +240,8 @@
     eye_n = iota((N, N), 0) == iota((N, N), 1)
     eye16 = onehot(eye_n)
 
-    wkv_near = spread(0, wkv_copies, wkv_spot)
     wq_copies = [to_peer(3, k, own_tall(wq, peers[k]), wq_spot(t, quarter)) for k in rest]
-
+    finish(0, wkv_begun, wkv_spot)
     own_copies[1].wait()
     landed(hid_copies)
     landed(inv_copies)
@@ -249,8 +253,9 @@
         inv_all[rows, :] = jnp.broadcast_to(inverse, (own, HD))
         normed[rows, :] = (hid_all[rows, :].astype(F32) * inverse * gain).astype(BF16)
     own_copies[2].wait()
-    landed(wkv_near)
     kvp_out[...] = nn(normed[...], wkv_all[...]).astype(BF16)
+
+    wq_begun = spread(3, wq_copies, wq_spot)
 
     def pair(p):
         return pl.ds(pl.multiple_of((p // 2) * (2 * HD), 256), 2 * HD)
@@ -260,10 +265,9 @@
     ]
     kvp_in[t] = kvp_out[:, pair(t)]
 
-    wq_near = spread(3, wq_copies, wq_spot)
     last16 = nn(last_hot, normed[...]).astype(BF16)
     own_copies[3].wait()
-    landed(wq_near)
+    finish(3, wq_begun, wq_spot)
     qp_out[...] = nn(last16, wq_all[...])
     qp_copies = [to_peer(6, k, qp_out.at[:, pair(peers[k])], qp_in.at[t]) for k in rest]
     qp_in[t] = qp_out[:, pair(t)]
@@ -289,6 +293,7 @@
     query_unit, query_inverse, query_rot = head_forward(query_raw, qg, cos_query, sin_query)
     query16 = query_rot.astype(BF16)
     scores = nt(query16, key16) / root
+    wo_begun = spread(6, wo_copies, wide_spot)
     weight = jnp.where(inside, jnp.exp(scores - shift), 0.0)
     probs = weight / jnp.sum(weight, axis=-1, keepdims=True)
     probs16 = probs.astype(BF16)
@@ -297,9 +302,8 @@
     my_attn = attn_all.at[:, block(t)]
     attn_copies = [to_peer(10, k, my_attn, my_attn) for k in rest]
 
-    wo_near = spread(6, wo_copies, wide_spot)
     own_copies[4].wait()
-    landed(wo_near)
+    finish(6, wo_begun, wide_spot)
     landed(attn_copies)
 
     resid = hid_last + nn(attn_all[...], wo_all[...])
@@ -457,7 +461,7 @@
     mean = jnp.sum(jnp.where(eye_n, row_sums[0:1, :], 0.0), axis=1, keepdims=True) / D
     inverse = inv_all[:, 0:1]
     landed(dkv_copies)
-    out_copies, local = [], []
+    out_copies, local, earlier = [], [], list(waits)
     FC = F // CHUNKS if F % (128 * CHUNKS) == 0 else F // 2
     for c in range(F // FC):
         span = slice(c * FC, (c + 1) * FC)
@@ -474,11 +478,12 @@
         )
         copy.start()
         local.append(copy)
-    landed(out_copies)
+    for copy in earlier:
+        copy.wait_send()
     for copy in local:
         copy.wait()
-    for copy in waits:
-        copy.wait_send()
+    for copy in out_copies:
+        copy.wait()
 
 
 def on_device(

time: 77 us -> 75 us (0.974)
  Pallas kernels: 72.2 us -> 70.6 us
    pallas_call x1, Pallas kernels: 72.2 us -> 70.6 us  [on_device(): pl.pallas_call(functools.partial(kernel, T, G), out_shape=(jax.ShapeDtype...]
where the time goes in v5:
time: 75 us; the launch traced here: 74.8 us
  Pallas kernels  70.6 us (94%)
  between operations  2.34 us (3%)
  local copies, waits for them, and re-layouts  1.87 us (2%)
    pallas_call x1, Pallas kernels, on_device(): pl.pallas_call(functools.partial(kernel, T, G), out_shape=(jax.ShapeDtype...  70.6 us
    unnamed x1, local copies, waits for them, and re-layouts  1.87 us

profile of v5, /device:TPU:0, one launch (start us, length us, event | category | flops | bytes accessed | tf_op | source)
XLA Modules:
  0.0 74.8 jit_solution(5241519857629918907)
XLA Ops:
  0.6 70.6 %shard_map.122 = (bf16[64,4096]{1,0:T(8,128)(2,1)}, f32[1,1]{1,0:T(1,128)}) custom-call(bf16[64,4096]{1,0:T(8,128)(2,1)} %hidden.1, s32[1,32]{1,0:T(1,128)} %lens_in.1, s32[1,64]{1,0:T(1,128)} %bitcast.10, s32[7,64]{1,0:T(8,128)} %bitcast.9, f32[1,4096]{1,0:T(1,128)} %bitcast.7, bf16[4096,128]{1,0:T(8,128)(2,1)} %wq.1, bf16[4096,128]{1,0:T(8,128)(2,1)} %wkv.1, ...), custom_call_target="tpu_custom_call" | custom-call | tf_op jit(solution)/shard_map/pallas_call | solution.py:542
  71.2 1.9 %copy.15 = bf16[64,4096]{1,0:T(8,128)(2,1)} copy(bf16[64,4096]{1,0:T(8,128)(2,1)} %get-tuple-element.8) | data formatting | bytes 1048576

commit v6 on v5

--- a/solution.py
+++ b/solution.py
@@ -73,7 +73,7 @@
     hidden, lens_in, positives_in, negatives_in, in_gain, wq, wkv, q_gain, k_gain, wo, out_gain,
     out, loss, lens, positives, negatives, gains, head_gains,
     hid_own, hid_all, inv_rows, inv_all, normed, wkv_all, wq_all, wo_all,
-    kvp_out, kvp_in, qp_out, qp_in, attn_all, embeds, logit_all, stats_all,
+    kvp_out, kvp_in, qp_out, qp_in, hid_seqs, attn_seqs, plain, embeds, logit_all, stats_all,
     dap_out, dap_in, dkv_all, dq_all, rows_all, addend, out16,
     local_sem, tsend, trecv, fsend, frecv, zsend, zrecv, psend, precv,
 ):
@@ -194,6 +194,40 @@
             near.append(pass_on(kind + 2, k, spot(sources[k], far_quarter), buddy))
         landed(near)
 
+    my_seqs = pl.ds(pl.multiple_of(g * S, S), S)
+
+    def chip_copy(row, index, spot):
+        copy = pltpu.make_async_remote_copy(
+            src_ref=spot, dst_ref=spot, send_sem=psend.at[row, index],
+            recv_sem=precv.at[row, index], device_id=(buddy, t), device_id_type=MESH,
+        )
+        copy.start()
+        waits.append(copy)
+        return copy
+
+    def gather_seqs(row, ref):
+        mine = ref.at[my_seqs]
+        copies = []
+        for k in range(1, Z):
+            far = lax.rem(zz + k, Z) * 2 + core
+            copy = pltpu.make_async_remote_copy(
+                src_ref=mine, dst_ref=mine, send_sem=zsend.at[row, k],
+                recv_sem=zrecv.at[row, k], device_id=(far, t), device_id_type=MESH,
+            )
+            copy.start()
+            waits.append(copy)
+            copies.append(copy)
+        return copies, [chip_copy(row, 0, mine)]
+
+    def share_seqs(row, ref, begun):
+        copies, shared = begun
+        for k in range(1, Z):
+            copies[k - 1].wait_recv()
+            origin = lax.rem(zz + Z - k, Z) * 2 + core
+            spot = ref.at[pl.ds(pl.multiple_of(origin * S, S), S)]
+            shared.append(chip_copy(row, k, spot))
+        return shared
+
     wkv_spot, wq_spot = tall_spot(wkv_all), tall_spot(wq_all)
     wkv_copies = [
         to_peer(1, k, own_tall(wkv, peers[k]), wkv_spot(t, quarter)) for k in rest
@@ -272,7 +306,8 @@
     qp_copies = [to_peer(6, k, qp_out.at[:, pair(peers[k])], qp_in.at[t]) for k in rest]
     qp_in[t] = qp_out[:, pair(t)]
     wo_copies = [to_peer(5, k, own_wide(peers[k]), wide_spot(t, quarter)) for k in rest]
-    hid_last = nn(last_hot, hid_all[...])
+    hid_seqs[my_seqs, :] = nn(last_hot, hid_all[...]).astype(BF16)
+    hid_begun = gather_seqs(0, hid_seqs)
     inverse_last = nn(last_hot.astype(F32), inv_all[...], EXACT)[:, 0:1]
 
     landed(kvp_copies)
@@ -298,40 +333,17 @@
     probs = weight / jnp.sum(weight, axis=-1, keepdims=True)
     probs16 = probs.astype(BF16)
     attn = nn(probs16, value16)
-    attn_all[:, block(t)] = jnp.where(even, attn[:S], attn[S:]).astype(BF16)
-    my_attn = attn_all.at[:, block(t)]
+    attn_seqs[my_seqs, block(t)] = jnp.where(even, attn[:S], attn[S:]).astype(BF16)
+    my_attn = attn_seqs.at[my_seqs, block(t)]
     attn_copies = [to_peer(10, k, my_attn, my_attn) for k in rest]
 
+    landed(attn_copies)
+    attn_begun = gather_seqs(1, attn_seqs)
+    finish(6, wo_begun, wide_spot)
     own_copies[4].wait()
-    finish(6, wo_begun, wide_spot)
-    landed(attn_copies)
-
-    resid = hid_last + nn(attn_all[...], wo_all[...])
-    my_seqs = pl.ds(pl.multiple_of(g * S, S), S)
-    embeds[my_seqs, :] = (resid * ogain).astype(BF16)
-    z_copies = []
-    for k in range(1, Z):
-        far = lax.rem(zz + k, Z) * 2 + core
-        copy = pltpu.make_async_remote_copy(
-            src_ref=embeds.at[my_seqs], dst_ref=embeds.at[my_seqs],
-            send_sem=zsend.at[k - 1], recv_sem=zrecv.at[k - 1],
-            device_id=(far, t), device_id_type=MESH,
-        )
-        copy.start()
-        waits.append(copy)
-        z_copies.append(copy)
-
-    def chip_copy(index, spot):
-        copy = pltpu.make_async_remote_copy(
-            src_ref=spot, dst_ref=spot, send_sem=psend.at[index], recv_sem=precv.at[index],
-            device_id=(buddy, t), device_id_type=MESH,
-        )
-        copy.start()
-        waits.append(copy)
-        return copy
-
-    shared = [chip_copy(0, embeds.at[my_seqs])]
-
+    hid_shared = share_seqs(0, hid_seqs, hid_begun)
+
+    resid = hid_seqs[my_seqs, :].astype(F32) + nn(attn_seqs[my_seqs, :], wo_all[...])
     E = G * S
     seq_of = iota((1, E), 1) % S
     passage = jnp.where(seq_of >= QDEV, (iota((1, E), 1) // S) * (S - QDEV) + seq_of - QDEV, -1)
@@ -355,19 +367,18 @@
     own_q = (row_s < QDEV) & (iota((S, Q), 1) == g * QDEV + row_s)
     own_p = iota((S, E), 1) == g * S + iota((S, E), 0)
     own_q16, own_p16 = onehot(own_q), onehot(own_p)
-    plain_gain = 1.0 / ogain
-
-    for k in range(1, Z):
-        z_copies[k - 1].wait_recv()
-        origin = lax.rem(zz + Z - k, Z) * 2 + core
-        shared.append(chip_copy(k, embeds.at[pl.ds(pl.multiple_of(origin * S, S), S)]))
-    landed(shared)
-
+
+    attn_shared = share_seqs(1, attn_seqs, attn_begun)
+    landed(hid_shared)
+    landed(attn_shared)
+
+    every = hid_seqs[...].astype(F32) + nn(attn_seqs[...], wo_all[...])
+    embeds[...] = (every * ogain).astype(BF16)
+    plain[...] = every.astype(BF16)
     queries = nn(pick_q, embeds[...]).astype(BF16)
     logit_all[t] = nt(queries, embeds[...])
     logit_copies = [to_peer(9, k, logit_all.at[t], logit_all.at[t]) for k in rest]
-    plain = (embeds[...].astype(F32) * plain_gain).astype(BF16)
-    plain_sq = jnp.sum(jnp.where(eye_e, nt(plain, plain), 0.0), axis=0, keepdims=True)
+    plain_sq = jnp.sum(jnp.where(eye_e, nt(plain[...], plain[...]), 0.0), axis=0, keepdims=True)
     scaled_sq = jnp.sum(
         jnp.where(eye_e, nt(embeds[...], embeds[...]), 0.0), axis=0, keepdims=True
     )
@@ -518,7 +529,9 @@
         pltpu.VMEM((T, N, 2 * HD), BF16),
         pltpu.VMEM((S, T * HD), F32),
         pltpu.VMEM((T, S, 2 * HD), F32),
-        pltpu.VMEM((S, T * HD), BF16),
+        pltpu.VMEM((G * S, F), BF16),
+        pltpu.VMEM((G * S, T * HD), BF16),
+        pltpu.VMEM((G * S, F), BF16),
         pltpu.VMEM((G * S, F), BF16),
         pltpu.VMEM((T, Q, G * S), F32),
         pltpu.VMEM((T, 8, G * S), F32),
@@ -534,10 +547,10 @@
         pltpu.SemaphoreType.DMA((14 + CHUNKS, T - 1)),
         pltpu.SemaphoreType.DMA((9, T - 1)),
         pltpu.SemaphoreType.DMA((9, T - 1)),
-        pltpu.SemaphoreType.DMA((Z,)),
-        pltpu.SemaphoreType.DMA((Z,)),
-        pltpu.SemaphoreType.DMA((Z,)),
-        pltpu.SemaphoreType.DMA((Z,)),
+        pltpu.SemaphoreType.DMA((2, Z)),
+        pltpu.SemaphoreType.DMA((2, Z)),
+        pltpu.SemaphoreType.DMA((2, Z)),
+        pltpu.SemaphoreType.DMA((2, Z)),
     ]
     d_hidden, loss = pl.pallas_call(
         functools.partial(kernel, T, G),

time: 75 us -> 71.3 us (0.951)
  Pallas kernels: 70.6 us -> 66.9 us
    pallas_call x1, Pallas kernels: 70.6 us -> 66.9 us  [on_device(): pl.pallas_call(functools.partial(kernel, T, G), out_shape=(jax.ShapeDtype...]
where the time goes in v6:
time: 71.3 us; the launch traced here: 71.1 us
  Pallas kernels  66.9 us (94%)
  between operations  2.34 us (3%)
  local copies, waits for them, and re-layouts  1.87 us (3%)
    pallas_call x1, Pallas kernels, on_device(): pl.pallas_call(functools.partial(kernel, T, G), out_shape=(jax.ShapeDtype...  66.9 us
    unnamed x1, local copies, waits for them, and re-layouts  1.87 us

profile of v6, /device:TPU:0, one launch (start us, length us, event | category | flops | bytes accessed | tf_op | source)
XLA Modules:
  0.0 71.1 jit_solution(15925046009295179353)
XLA Ops:
  0.6 66.9 %shard_map.122 = (bf16[64,4096]{1,0:T(8,128)(2,1)}, f32[1,1]{1,0:T(1,128)}) custom-call(bf16[64,4096]{1,0:T(8,128)(2,1)} %hidden.1, s32[1,32]{1,0:T(1,128)} %lens_in.1, s32[1,64]{1,0:T(1,128)} %bitcast.10, s32[7,64]{1,0:T(8,128)} %bitcast.9, f32[1,4096]{1,0:T(1,128)} %bitcast.7, bf16[4096,128]{1,0:T(8,128)(2,1)} %wq.1, bf16[4096,128]{1,0:T(8,128)(2,1)} %wkv.1, ...), custom_call_target="tpu_custom_call" | custom-call | tf_op jit(solution)/shard_map/pallas_call | solution.py:555
  67.5 1.9 %copy.15 = bf16[64,4096]{1,0:T(8,128)(2,1)} copy(bf16[64,4096]{1,0:T(8,128)(2,1)} %get-tuple-element.8) | data formatting | bytes 1048576

commit v7 on v6

--- a/solution.py
+++ b/solution.py
@@ -277,18 +277,19 @@
     wq_copies = [to_peer(3, k, own_tall(wq, peers[k]), wq_spot(t, quarter)) for k in rest]
     finish(0, wkv_begun, wkv_spot)
     own_copies[1].wait()
-    landed(hid_copies)
-    landed(inv_copies)
-    for s in slots:
-        rows = slice(s * own, (s + 1) * own)
+    own_copies[2].wait()
+    for k, source in [(None, t)] + list(enumerate(sources)):
+        if k is not None:
+            inv_copies[k].wait_recv()
+            hid_copies[k].wait_recv()
+        rows = pl.ds(pl.multiple_of(source * own, own), own)
         inverse = jnp.sum(
-            jnp.where(diagonal, inv_rows[s, 0:1, :], 0.0), axis=1, keepdims=True
+            jnp.where(diagonal, inv_rows[source, 0:1, :], 0.0), axis=1, keepdims=True
         )
         inv_all[rows, :] = jnp.broadcast_to(inverse, (own, HD))
-        normed[rows, :] = (hid_all[rows, :].astype(F32) * inverse * gain).astype(BF16)
-    own_copies[2].wait()
-    kvp_out[...] = nn(normed[...], wkv_all[...]).astype(BF16)
-
+        part = (hid_all[rows, :].astype(F32) * inverse * gain).astype(BF16)
+        normed[rows, :] = part
+        kvp_out[rows, :] = nn(part, wkv_all[...]).astype(BF16)
     wq_begun = spread(3, wq_copies, wq_spot)
 
     def pair(p):

time: 71.3 us -> 72.2 us (1.013)
  Pallas kernels: 66.9 us -> 67.8 us
    pallas_call x1, Pallas kernels: 66.9 us -> 67.8 us  [on_device(): pl.pallas_call(functools.partial(kernel, T, G), out_shape=(jax.ShapeDtype...]
where the time goes in v7:
time: 72.2 us; the launch traced here: 72 us
  Pallas kernels  67.8 us (94%)
  between operations  2.34 us (3%)
  local copies, waits for them, and re-layouts  1.87 us (3%)
    pallas_call x1, Pallas kernels, on_device(): pl.pallas_call(functools.partial(kernel, T, G), out_shape=(jax.ShapeDtype...  67.8 us
    unnamed x1, local copies, waits for them, and re-layouts  1.87 us

profile of v7, /device:TPU:0, one launch (start us, length us, event | category | flops | bytes accessed | tf_op | source)
XLA Modules:
  0.0 72.0 jit_solution(854258343509932628)
XLA Ops:
  0.6 67.8 %shard_map.122 = (bf16[64,4096]{1,0:T(8,128)(2,1)}, f32[1,1]{1,0:T(1,128)}) custom-call(bf16[64,4096]{1,0:T(8,128)(2,1)} %hidden.1, s32[1,32]{1,0:T(1,128)} %lens_in.1, s32[1,64]{1,0:T(1,128)} %bitcast.10, s32[7,64]{1,0:T(8,128)} %bitcast.9, f32[1,4096]{1,0:T(1,128)} %bitcast.7, bf16[4096,128]{1,0:T(8,128)(2,1)} %wq.1, bf16[4096,128]{1,0:T(8,128)(2,1)} %wkv.1, ...), custom_call_target="tpu_custom_call" | custom-call | tf_op jit(solution)/shard_map/pallas_call | solution.py:556
  68.5 1.9 %copy.15 = bf16[64,4096]{1,0:T(8,128)(2,1)} copy(bf16[64,4096]{1,0:T(8,128)(2,1)} %get-tuple-element.8) | data formatting | bytes 1048576
